TPU v7x, 256 devices: a whole 4x4x8 slice. The times are simulated.
256 devices in a mesh: dp: 32 (over y, z), tensor: 8 (over x, core).
Axes of the slice: x: 4, y: 4, z: 8, core: 2. Of those that a mesh axis runs over, the one named last changes fastest.
Arguments:
- queries: bfloat16 [4096, 5120], P('dp', 'tensor'), may hold values from -64 to 64
- response_key_value: bfloat16 [4096, 2048], P('dp', 'tensor'), may hold values from -6 to 6
- prompt_kv: bfloat16 [32, 8, 64, 2048], P('dp', None, None, 'tensor'), may hold values from -6 to 6
- prompt_group: int32 [32, 8], P('dp'), may hold values from 0 to 7, as said below
- response_order: int32 [32], replicated, may hold values from 0 to 31, as said below
- live_blocks: int32 [32], P('dp'), may hold values from 1 to 1
- out_weight: bfloat16 [5120, 5120], P('tensor'), may hold values from -0.078125 to 0.078125
- grad_out: bfloat16 [4096, 5120], P('dp', 'tensor'), may hold values from -6 to 6
Outputs:
- grad_queries: bfloat16 [4096, 5120], P('dp', 'tensor')
- grad_resp_kv: bfloat16 [4096, 2048], P('dp', 'tensor')
- grad_prompt_kv: bfloat16 [32, 8, 64, 2048], P('dp', None, None, 'tensor')
Inputs may be any that keep to these rules, and one draw needn't show every extreme that they name: `prompt_group`: each row holds every group number once. `response_order`: every response number appears once; response r belongs to group r // 4.
All inputs are finite; a program needn't handle non-finite values.
Results may differ from a plain program's by a relative error of at most 0.012.
Values may be sent and summed in bfloat16 or wider, within the bound.
A program may use at most 64 MiB of HBM per device.

v0:
```python
import math

import jax
import jax.numpy as jnp
from jax import lax
from jax.sharding import PartitionSpec as P

HEAD_SIZE = 128
QB = 128


def attend_block(
    first_row, query_block, grad_block, keys_prompt, vals_prompt, keys_resp, vals_resp, score_scale
):
    score_prompt = (
        jnp.einsum("thd,kd->htk", query_block, keys_prompt, preferred_element_type=jnp.float32)
        * score_scale
    )
    score_resp = (
        jnp.einsum("thd,kd->htk", query_block, keys_resp, preferred_element_type=jnp.float32)
        * score_scale
    )
    query_pos = first_row + lax.broadcasted_iota(jnp.int32, score_resp.shape, 1)
    key_pos = lax.broadcasted_iota(jnp.int32, score_resp.shape, 2)
    score_resp = jnp.where(key_pos <= query_pos, score_resp, -jnp.inf)
    row_max = jnp.maximum(
        jnp.max(score_prompt, axis=2, keepdims=True), jnp.max(score_resp, axis=2, keepdims=True)
    )
    expo_prompt = jnp.exp(score_prompt - row_max)
    expo_resp = jnp.exp(score_resp - row_max)
    denominator = jnp.sum(expo_prompt, axis=2, keepdims=True) + jnp.sum(
        expo_resp, axis=2, keepdims=True
    )
    prob_prompt = expo_prompt / denominator
    prob_resp = expo_resp / denominator
    weight_prompt = prob_prompt.astype(jnp.bfloat16)
    weight_resp = prob_resp.astype(jnp.bfloat16)
    attended = jnp.einsum(
        "htk,kd->thd", weight_prompt, vals_prompt, preferred_element_type=jnp.float32
    ) + jnp.einsum("htk,kd->thd", weight_resp, vals_resp, preferred_element_type=jnp.float32)
    row_delta = jnp.sum(grad_block.astype(jnp.float32) * attended, axis=2).T
    back_prompt = jnp.einsum(
        "thd,kd->htk", grad_block, vals_prompt, preferred_element_type=jnp.float32
    )
    back_resp = jnp.einsum("thd,kd->htk", grad_block, vals_resp, preferred_element_type=jnp.float32)
    slope_prompt = (prob_prompt * (back_prompt - row_delta[:, :, None])).astype(jnp.bfloat16)
    slope_resp = (prob_resp * (back_resp - row_delta[:, :, None])).astype(jnp.bfloat16)
    grad_query = (
        jnp.einsum("htk,kd->thd", slope_prompt, keys_prompt, preferred_element_type=jnp.float32)
        + jnp.einsum("htk,kd->thd", slope_resp, keys_resp, preferred_element_type=jnp.float32)
    ) * score_scale
    gkey_prompt = (
        jnp.einsum("htk,thd->kd", slope_prompt, query_block, preferred_element_type=jnp.float32)
        * score_scale
    )
    gval_prompt = jnp.einsum(
        "htk,thd->kd", weight_prompt, grad_block, preferred_element_type=jnp.float32
    )
    gkey_resp = (
        jnp.einsum("htk,thd->kd", slope_resp, query_block, preferred_element_type=jnp.float32)
        * score_scale
    )
    gval_resp = jnp.einsum(
        "htk,thd->kd", weight_resp, grad_block, preferred_element_type=jnp.float32
    )
    return (grad_query, gkey_prompt, gval_prompt, gkey_resp, gval_resp)


def body(
    queries,
    response_key_value,
    prompt_kv,
    prompt_group,
    response_order,
    live_blocks,
    out_weight,
    grad_out,
):
    dev_count = lax.axis_size("dp")
    response_rows = queries.shape[0]
    query_width = queries.shape[1]
    key_value_width = response_key_value.shape[1]
    head_dim = HEAD_SIZE
    kv_heads = key_value_width // (2 * head_dim)
    group_count = query_width // (kv_heads * head_dim)
    groups = prompt_kv.shape[1]
    block_rows = prompt_kv.shape[2]
    prompt_length = dev_count * block_rows
    score_scale = 1.0 / math.sqrt(head_dim)
    attention_gradient = lax.dot_general(
        lax.all_gather(grad_out, "tensor", axis=1, tiled=True),
        out_weight,
        (((1,), (1,)), ((), ())),
        preferred_element_type=jnp.float32,
    )
    live_rows = live_blocks[0] * QB
    positions = lax.broadcasted_iota(jnp.int32, (response_rows, 1), 0)
    attention_gradient = jnp.where(positions < live_rows, attention_gradient, 0.0).astype(
        jnp.bfloat16
    )
    group_of = response_order // 4
    every_block, every_group = (
        lax.all_gather(prompt_kv, "dp", axis=0, tiled=True),
        lax.all_gather(prompt_group, "dp", axis=0, tiled=True),
    )
    my_index = lax.axis_index("dp")
    lane_index = lax.broadcasted_iota(jnp.int32, (dev_count,), 0)
    my_group = jnp.sum(jnp.where(lane_index == my_index, group_of, 0))
    selector = (every_group == my_group).astype(jnp.bfloat16)
    chosen = jnp.einsum(
        "sc,scx->sx",
        selector,
        every_block.reshape(dev_count, groups, block_rows * key_value_width),
        preferred_element_type=jnp.float32,
    )
    received = chosen.astype(jnp.bfloat16).reshape(prompt_length, key_value_width)
    loop_limit = response_rows // QB
    resp_parts = []
    prompt_parts = []
    keys_prompt = received[:, 0:head_dim]
    vals_prompt = received[:, head_dim : 2 * head_dim]
    keys_resp = response_key_value[:, 0:head_dim]
    vals_resp = response_key_value[:, head_dim : 2 * head_dim]
    query_head = queries.reshape(response_rows, group_count, head_dim)
    grad_head = attention_gradient.reshape(response_rows, group_count, head_dim)

    def block_step(block_index, running_state):
        grad_q, gkey_prompt, gval_prompt, gkey_resp, gval_resp = running_state
        first_row = block_index * QB
        grad_piece, key_piece, val_piece, rkey_piece, rval_piece = attend_block(
            first_row,
            query_head,
            grad_head,
            keys_prompt,
            vals_prompt,
            keys_resp,
            vals_resp,
            score_scale,
        )
        grad_q = grad_piece.astype(jnp.bfloat16)
        return (
            grad_q,
            gkey_prompt + key_piece,
            gval_prompt + val_piece,
            gkey_resp + rkey_piece,
            gval_resp + rval_piece,
        )

    initial = (
        jnp.zeros((response_rows, group_count, head_dim), jnp.bfloat16),
        jnp.zeros((prompt_length, head_dim), jnp.float32),
        jnp.zeros((prompt_length, head_dim), jnp.float32),
        jnp.zeros((response_rows, head_dim), jnp.float32),
        jnp.zeros((response_rows, head_dim), jnp.float32),
    )
    grad_q, gkey_prompt, gval_prompt, gkey_resp, gval_resp = lax.fori_loop(
        0, loop_limit, block_step, initial
    )
    query_parts = grad_q.reshape(response_rows, group_count * head_dim)
    resp_parts.append(gkey_resp)
    resp_parts.append(gval_resp)
    prompt_parts.append(gkey_prompt)
    prompt_parts.append(gval_prompt)
    grad_resp_kv = jnp.concatenate(resp_parts, axis=1).astype(jnp.bfloat16)
    prompt_terms = jnp.concatenate(prompt_parts, axis=1).reshape(
        dev_count, block_rows, key_value_width
    )
    returned = lax.all_to_all(prompt_terms, "dp", split_axis=0, concat_axis=0, tiled=True)
    owners = (prompt_group[0][:, None] == group_of[None, :]).astype(jnp.float32)
    summed = jnp.dot(
        owners,
        returned.reshape(dev_count, block_rows * key_value_width),
        precision=lax.Precision.HIGHEST,
        preferred_element_type=jnp.float32,
    )
    grad_prompt_kv = summed.reshape(1, groups, block_rows, key_value_width).astype(jnp.bfloat16)
    return (query_parts, grad_resp_kv, grad_prompt_kv)


def solution(mesh):
    return jax.shard_map(
        body,
        mesh=mesh,
        in_specs=(
            P("dp", "tensor"),
            P("dp", "tensor"),
            P("dp", None, None, "tensor"),
            P("dp", None),
            P(),
            P("dp"),
            P("tensor", None),
            P("dp", "tensor"),
        ),
        out_specs=(P("dp", "tensor"), P("dp", "tensor"), P("dp", None, None, "tensor")),
        check_vma=False,
    )
```

profile of v0, /device:TPU:2, one launch (start us, length us, event | category | flops | bytes accessed | tf_op | source)
XLA Modules:
  0.0 239.6 jit_solution(8302541494372351980)
XLA Ops:
  7.2 0.0 all-gather.6.cloned.1.call-start
  7.2 0.7 all-gather.6.cloned.1.call-update
  7.9 0.0 all-gather.4.cloned.1.call-start
  7.9 0.7 all-gather.4.cloned.1.call-update
  9.3 42.0 %all-gather = s32[32,1,8]{2,1,0:T(1,128)S(1)} all-gather(s32[1,1,8]{2,1,0:T(1,128)} %bitcast.163), channel_id=1, replica_groups=mesh['dp'=32,'tensor'=8] {'dp'}, dimensions={0}, use_global_device_ids=true | all-gather | bytes 1056 | tf_op jit(solution)/shard_map/all_gather | solution.py:104
  51.3 0.1 copy.63
  51.4 1.3 fusion.52
  52.7 0.6 compare_bitcast_fusion
  53.3 0.1 copy.89
  53.5 1.1 copy.64
  54.6 1.0 fusion.57
  55.5 0.0 all-gather.6.cloned.1.call-done
  55.6 5.4 %fusion.31 = bf16[128,640]{1,0:T(8,128)(2,1)S(1)} fusion(bf16[128,5120]{1,0:T(8,128)(2,1)} %all-gather.6.cloned.1.call-done, bf16[640,5120]{1,0:T(8,128)(2,1)} %param.14, pred[128]{0:T(512)(128)(4,1)S(1)} %iota_compare_fusion.1), kind=kOutput, calls=%fused_computation.38 | convolution fusion | flops 839024640 | bytes 8028288 | tf_op jit(solution)/shard_map/dot_general | solution.py:90
  61.0 0.2 copy.67
  61.1 79.2 %all-gather.4.cloned.1.call-done = bf16[32,8,64,256]{3,2,1,0:T(8,128)(2,1)} async-done(((bf16[1,8,64,256]{3,2,1,0:T(8,128)(2,1)}), bf16[32,8,64,256]{3,2,1,0:T(8,128)(2,1)}) %all-gather.4.cloned.1.call-update) | async-done | bytes 8388624 | tf_op jit(solution)/shard_map/all_gather | solution.py:103
  140.3 13.5 %reshape.53 = bf16[32,8,16384]{2,1,0:T(8,128)(2,1)} reshape(bf16[32,8,64,256]{3,2,1,0:T(8,128)(2,1)} %all-gather.4.cloned.1.call-done) | data formatting | bytes 16777216 | tf_op jit(solution)/shard_map/reshape | solution.py:113
  153.8 5.7 %fusion.58 = bf16[32,1,16384]{2,1,0:T(2,128)(2,1)S(1)} fusion(pred[32,8,1]{1,2,0:T(4,128)(4,1)S(1)} %copy.89, bf16[32,8,16384]{2,1,0:T(8,128)(2,1)} %reshape.53), kind=kOutput, calls=%fused_computation.76 | convolution fusion | flops 8388608 | bytes 9437440 | tf_op jit(solution)/shard_map/sc,scx->sx/dot_general | solution.py:110
  159.5 1.2 copy.127
  160.7 0.5 reshape.54
  161.2 0.0 copy-start
  161.2 0.8 bitcast_reduce_fusion
  162.1 0.1 fusion.38
  162.1 0.9 fusion.4
  163.0 0.0 copy-done
  163.0 1.3 fusion.23
  164.4 0.0 copy-start.2
  164.4 0.0 copy-start.1
  164.4 1.3 convolution_bitcast_fusion
  165.7 0.0 copy-done.2
  165.7 0.2 fusion.32
  166.0 0.0 copy-done.1
  166.0 1.5 fusion.1
  167.5 1.0 fusion.5
  168.5 1.5 pad_maximum_fusion
  170.0 2.9 %copy.84 = f32[2048,256]{1,0:T(8,128)} copy(f32[2048,256]{0,1:T(8,128)} %pad_maximum_fusion) | data formatting | bytes 4194304 | tf_op jit(solution)/shard_map/concatenate | solution.py:165
  172.9 0.0 copy-start.3
  172.9 6.1 %all-to-all-start = ((f32[32,64,256]{2,1,0:T(8,128)}), f32[32,64,256]{2,1,0:T(8,128)}, u32[]{:S(2)}, u32[]{:S(2)}) async-start(f32[32,64,256]{2,1,0:T(8,128)} %bitcast.151), calls=%async_computation | async-start | bytes 4194304 | tf_op jit(solution)/shard_map/all_to_all | solution.py:168
  179.0 0.2 fusion.30
  179.2 0.2 fusion.35
  179.4 0.2 fusion.34
  179.7 0.7 copy.87
  180.4 1.6 convolution_bitcast_fusion.2
  182.1 0.2 fusion.29
  182.3 0.8 copy.86
  183.1 45.4 %all-to-all-done = f32[32,64,256]{2,1,0:T(8,128)} async-done(((f32[32,64,256]{2,1,0:T(8,128)}), f32[32,64,256]{2,1,0:T(8,128)}, u32[]{:S(2)}, u32[]{:S(2)}) %all-to-all-start) | async-done | bytes 2097184 | tf_op jit(solution)/shard_map/all_to_all | solution.py:168
  228.6 0.0 copy-done.3
  228.6 3.4 %fusion.26 = bf16[1,8,64,256]{3,1,2,0:T(8,128)(2,1)S(1)} fusion(s32[32]{0:T(128)S(1)} %get-tuple-element.38, s32[8]{0:T(128)S(1)} %bitcast.164, f32[4,8,64,256]{3,2,1,0:T(8,128)} %bitcast.39), kind=kOutput, calls=%fused_computation.34 | convolution fusion | flops 50462976 | bytes 2359456 | tf_op jit(solution)/shard_map/dot_general | solution.py:170
  232.0 0.8 copy.88
  (4 shorter events, 0.0 us)
Async XLA Ops:
  7.2 48.4 %all-gather.6.cloned.1.call-start = ((), (), s32[]{:S(2)}) async-start(), calls=%async_computation.2 | async-start | bytes 1474560 | tf_op jit(solution)/shard_map/all_gather | solution.py:91
  7.9 132.5 %all-gather.4.cloned.1.call-start = ((), (), s32[]{:S(2)}) async-start(), calls=%async_computation.1 | async-start | bytes 8650752 | tf_op jit(solution)/shard_map/all_gather | solution.py:103
  161.2 1.8 copy-start
  164.4 1.3 copy-start.2
  164.4 1.6 copy-start.1
  172.9 55.6 %copy-start.3 = (s32[1,8]{1,0:T(1,128)S(1)}, s32[1,8]{1,0:T(1,128)}, u32[]{:S(2)}) copy-start(s32[1,8]{1,0:T(1,128)} %param.11) | copy-start | bytes 100
  172.9 55.6 %all-to-all-start = ((f32[32,64,256]{2,1,0:T(8,128)}), f32[32,64,256]{2,1,0:T(8,128)}, u32[]{:S(2)}, u32[]{:S(2)}) async-start(f32[32,64,256]{2,1,0:T(8,128)} %bitcast.151), calls=%async_computation | async-start | bytes 4194304 | tf_op jit(solution)/shard_map/all_to_all | solution.py:168
Sparse Core Ops, SparseCore 0:
  9.8 27.8 all-gather.5
  40.4 99.9 all-gather.3
where the time goes:
time: 240 us
  waiting for transfers between devices  126 us (52%)
  blocking collectives  42 us (18%)
  matrix products  24.2 us (10%)
  local copies, waits for them, and re-layouts  21.8 us (9%)
  between operations  14.9 us (6%)
  starting transfers between devices  6.15 us (3%)
  other arithmetic  4.41 us (2%)
    all_gather x1, waiting for transfers between devices, body(): lax.all_gather(prompt_kv, 'dp', axis=0, tiled=True)  79.2 us
    all_to_all x1, waiting for transfers between devices, body(): lax.all_to_all(prompt_terms, 'dp', split_axis=0, concat_axis=0, tiled=True)  45.4 us
    all_gather x1, blocking collectives, body(): lax.all_gather(prompt_group, 'dp', axis=0, tiled=True)  42 us
    reshape x1, local copies, waits for them, and re-layouts, body(): every_block.reshape(dev_count, groups, block_rows * key_value_width)  13.5 us
    all_to_all x1, starting transfers between devices, body(): lax.all_to_all(prompt_terms, 'dp', split_axis=0, concat_axis=0, tiled=True)  6.07 us
    dot_general x1, matrix products, body(): jnp.einsum('sc,scx->sx', selector, every_block.reshape(dev_count, groups,...  5.69 us
    dot_general x1, matrix products, body(): lax.dot_general(lax.all_gather(grad_out, 'tensor', axis=1, tiled=True), o...  5.4 us
  transfers between devices with their start and end apart: 3, of which 2 were waited for; matrix products, arithmetic and copies ran while one was open for 6% of the time, Pallas kernels for 0%

commit v1 on v0

v1 whole, which is shorter than its diff:
```python
import math

import jax
import jax.numpy as jnp
from jax import lax
from jax.experimental import pallas as pl
from jax.experimental.pallas import tpu as pltpu
from jax.sharding import PartitionSpec as P

HEAD = 128
HEADS = 5
WIDTH = HEAD * HEADS
TOKENS = 128
BLOCK = 64
GROUPS = 8
NY, NZ, NX = 4, 8, 4
PIECES = 8
KEYS = NZ * BLOCK
SCALE = 1.0 / math.sqrt(HEAD)
EXP2_SCALE = SCALE * math.log2(math.e)
N_COPIES = 80
MESH = pl.DeviceIdType.MESH
BF16, F32 = jnp.bfloat16, jnp.float32


def mm(a, b):
    return jnp.dot(a, b, preferred_element_type=F32)


def mm_t(a, b):
    return lax.dot_general(a, b, (((1,), (1,)), ((), ())), preferred_element_type=F32)


def fold(x, op):
    return op(x.reshape(x.shape[0] // 8, 8, x.shape[1]), axis=0)


def each(count, step):
    def run(index, carry):
        step(index)
        return carry

    lax.fori_loop(0, count, run, 0)


def each_pair(count, step):
    def both(index):
        step(2 * index)
        step(2 * index + 1)

    each(count // 2, both)


def kernel(
    q_ref, rkv_ref, pkv_ref, pg_ref, ro_ref, lb_ref, w_ref, go_ref,
    oq_ref, or_ref, op_ref,
    q_v, rkv_v, pkv_v, go_v, oq_v, or_v, op_v,
    w_v, gox, gos, g_own, q_buf, g_buf, qs, gs,
    own, r1, st2, st3, st4, kv,
    e_buf, e_own, p_buf, p_own, dp_buf, dp_own, ds_buf, ds_own,
    tops, sums, dots, coef, shares, row_delta, stat_out, stat_in, del_out, del_in,
    s2, s3, s4, q2, q3, q4, summed, back_in, dkv, dq_send, dq_recv,
    marks, in_sem, out_sem, w_sem, send_sem, recv_sem,
):
    dp = lax.axis_index("dp")
    tensor = lax.axis_index("tensor")
    y, z = dp // NZ, dp % NZ
    x, core = tensor // 2, tensor % 2

    def at_z(step):
        return (y * NZ + (z + step + NZ) % NZ, tensor)

    def at_y(step):
        return (((y + step + NY) % NY) * NZ + z, tensor)

    def at_x(step):
        return (dp, ((x + step + NX) % NX) * 2 + core)

    sibling = (dp, x * 2 + 1 - core)

    numbers = {}
    started = []

    def remote(name, src, dst, device):
        n = numbers.setdefault(name, len(numbers))
        return pltpu.make_async_remote_copy(
            src_ref=src, dst_ref=dst, send_sem=send_sem.at[n], recv_sem=recv_sem.at[n],
            device_id=device, device_id_type=MESH,
        )

    def go(copy):
        copy.start()
        started.append(copy)

    barrier = pltpu.get_barrier_semaphore()
    partners = [at_z(step) for step in (1, -1, 2, -2, 3, -3)]
    partners += [at_y(1), at_y(2), at_y(3), at_x(1), at_x(-1), sibling]
    for partner in partners:
        pl.semaphore_signal(barrier, inc=1, device_id=partner, device_id_type=MESH)
    in_copies = [
        pltpu.make_async_copy(src, dst, in_sem.at[n])
        for n, (src, dst) in enumerate(
            [(pkv_ref, pkv_v), (go_ref, go_v), (q_ref, q_v), (rkv_ref, rkv_v)]
        )
    ]
    for copy in in_copies:
        copy.start()

    w_copies = []
    for r in range(NX):
        for other in range(2):
            piece = ((x + r) % NX) * 2 + (core if other == 0 else 1 - core)
            copy = pltpu.make_async_copy(
                w_ref.at[:, pl.ds(pl.multiple_of(piece * WIDTH, WIDTH), WIDTH)],
                w_v.at[r * 2 + other], w_sem.at[r * 2 + other],
            )
            copy.start()
            w_copies.append(copy)

    in_copies[0].wait()
    for g in range(GROUPS):
        slot = jnp.int32(0)
        for c in range(GROUPS):
            slot = jnp.where(pg_ref[0, c] == g, c, slot)
        block = pkv_v[0, slot]
        own[0, g] = block[:, :HEAD]
        own[1, g] = block[:, HEAD:]
    for copy in in_copies[1:]:
        copy.wait()
    pl.semaphore_wait(barrier, len(partners))

    def hop(step, c, d):
        sign = 1 if d == 0 else -1
        src, dst, device = {
            1: (own.at[c], r1[c][d], at_z(sign)),
            2: (st2.at[c, d], kv.at[c, :, pl.ds((3 + d) * BLOCK, BLOCK)], at_z(sign)),
            3: (st3.at[c, d], kv.at[c, :, pl.ds((5 + d) * BLOCK, BLOCK)], at_z(2 * sign)),
            4: (
                st4.at[c, d], kv.at[c, pl.ds(2 * d, 2), pl.ds(7 * BLOCK, BLOCK)],
                at_z(3 * sign),
            ),
        }[step]
        return remote(("hop", step, c, d), src, dst, device)

    half = TOKENS // 2

    def ring_copy(name, src, buf, before, after, way, part):
        rows = pl.ds(part * half, half)
        dst = buf.at[1 if way == 0 else 3, rows]
        return remote((name, way, part), src.at[rows], dst, before if way == 0 else after)

    def ring_pass(name, buf, before, after, way):
        rows = pl.ds(way * half, half)
        return remote(
            (name, way, 2), buf.at[1 if way == 0 else 3, rows], buf.at[2, rows],
            before if way == 0 else after,
        )

    def ring_first(*ring):
        for turn in range(2):
            for way in range(2):
                go(ring_copy(*ring, way, way if turn == 0 else 1 - way))

    def ring_second(name, src, buf, before, after):
        for way in range(2):
            ring_copy(name, src, buf, before, after, way, way).wait_recv()
            go(ring_pass(name, buf, before, after, way))

    def ring_rest(name, src, buf, before, after):
        for way in range(2):
            ring_copy(name, src, buf, before, after, way, 1 - way).wait_recv()

    def ring_last(name, src, buf, before, after):
        for way in range(2):
            ring_pass(name, buf, before, after, way).wait_recv()

    x_ring = ("x", go_v, gox, at_x(-1), at_x(1))
    q_ring = ("q", q_v, q_buf, at_y(-1), at_y(1))
    g_ring = ("g", g_own, g_buf, at_y(-1), at_y(1))

    def share(r):
        src = go_v if r == 0 else gox.at[r]
        return remote(("share", r), src, gos.at[r], sibling)

    ring_first(*x_ring)
    for d in range(2):
        go(hop(1, 0, d))
    go(share(0))
    ring_first(*q_ring)

    groups = {
        step: [ro_ref[((y + j) % NY) * NZ + (z + step + NZ) % NZ] // 4 for j in range(NY)]
        for step in range(-3, 4)
    }
    my_groups = groups[0]

    def relay(c):
        for d in range(2):
            sign = 1 if d == 0 else -1
            hop(1, c, d).wait_recv()
            for i in range(2):
                st4[c, d, i] = r1[c][d][groups[3 * sign][2 * d + i]]
            go(hop(4, c, d))
            for j in range(NY):
                st3[c, d, j] = r1[c][d][groups[2 * sign][j]]
            go(hop(3, c, d))
            for j in range(NY):
                st2[c, d, j] = r1[c][d][groups[sign][j]]
            go(hop(2, c, d))

    def stack_heads(raw, stacked, j):
        for h in range(HEADS):
            stacked[j, h * HEAD : (h + 1) * HEAD, :] = raw[:, h * HEAD : (h + 1) * HEAD]

    levels = [(0, 1), (1, 2), (3, 2), (5, 3)]

    def weigh(s):
        top = jnp.max(fold(s, jnp.max), axis=0, keepdims=True)
        e = jnp.exp2((s - top) * EXP2_SCALE)
        return top, e, jnp.sum(fold(e, jnp.sum), axis=0, keepdims=True)

    def scores(j, level):
        first, count = levels[level][0] * BLOCK, levels[level][1] * BLOCK
        top, e, total = weigh(mm_t(kv[0, j, first : first + count, :], qs[j]))
        e_buf[j, first : first + count, :] = e.astype(BF16)
        tops[j, level : level + 1, :] = top
        sums[j, level : level + 1, :] = total

    def slopes(j, level):
        first, count = levels[level][0] * BLOCK, levels[level][1] * BLOCK
        terms = mm_t(kv[1, j, first : first + count, :], gs[j])
        dp_buf[j, first : first + count, :] = terms
        products = terms * e_buf[j, first : first + count, :].astype(F32)
        dots[j, level : level + 1, :] = jnp.sum(fold(products, jnp.sum), axis=0, keepdims=True)

    def take(c, level):
        for j in range(NY):
            g = my_groups[j]
            if level == 0:
                kv[c, j, 0:BLOCK, :] = own[c, g]
            else:
                kv[c, j, BLOCK : 2 * BLOCK, :] = r1[c][0][g]
                kv[c, j, 2 * BLOCK : 3 * BLOCK, :] = r1[c][1][g]

    def arrived(c, steps):
        for step in steps:
            for d in range(2):
                hop(step, c, d).wait_recv()

    def project(piece, block):
        w_copies[piece].wait()
        return mm_t(w_v[piece], block[...])

    grad = project(0, go_v)
    for d in range(2):
        go(hop(1, 1, d))
    tops[...] = jnp.full(tops.shape, -jnp.inf, F32)
    sums[...] = jnp.zeros(sums.shape, F32)
    dots[...] = jnp.zeros(dots.shape, F32)
    del_out[...] = jnp.zeros(del_out.shape, F32)
    share(0).wait_recv()
    grad = grad + project(1, gos.at[0])

    stack_heads(q_v[...], qs, 0)
    s = mm_t(rkv_v[:, :HEAD], qs[0])
    key_pos = lax.broadcasted_iota(jnp.int32, s.shape, 0)
    query_pos = lax.broadcasted_iota(jnp.int32, s.shape, 1) % TOKENS
    top, e, total = weigh(jnp.where(key_pos <= query_pos, s, -jnp.inf))
    e_own[...] = e.astype(BF16)
    tops[0, 5:6, :] = top
    sums[0, 5:6, :] = total

    ring_second(*x_ring)
    ring_rest(*x_ring)
    go(share(1))
    go(share(3))
    relay(0)
    ring_second(*q_ring)
    grad = grad + project(2, gox.at[1])
    grad = grad + project(6, gox.at[3])
    ring_last(*x_ring)
    go(share(2))
    share(1).wait_recv()
    grad = grad + project(3, gos.at[1])
    share(3).wait_recv()
    grad = grad + project(7, gos.at[3])
    relay(1)
    grad = grad + project(4, gox.at[2])
    share(2).wait_recv()
    grad = grad + project(5, gos.at[2])
    column = lax.broadcasted_iota(jnp.int32, grad.shape, 1)
    grad = jnp.where(column < lb_ref[0] * TOKENS, grad, 0.0).astype(BF16)
    for h in range(HEADS):
        head = grad[h * HEAD : (h + 1) * HEAD, :].T
        gs[0, h * HEAD : (h + 1) * HEAD, :] = head
        g_own[:, h * HEAD : (h + 1) * HEAD] = head
    ring_first(*g_ring)
    ring_rest(*q_ring)
    for level in range(2):
        take(0, level)
        take(1, level)
    for j in (1, 3):
        stack_heads(q_buf[j], qs, j)
    for j in (0, 1, 3):
        scores(j, 0)
        scores(j, 1)
    ring_last(*q_ring)
    stack_heads(q_buf[2], qs, 2)
    scores(2, 0)
    scores(2, 1)
    arrived(0, (2,))
    each(NY, lambda j: scores(j, 2))
    ring_second(*g_ring)
    arrived(0, (3, 4))
    each(NY, lambda j: scores(j, 3))

    for j in range(NY):
        top = jnp.max(tops[j], axis=0, keepdims=True)
        share_of = jnp.exp2((tops[j] - top) * EXP2_SCALE)
        shares[j] = share_of
        stat_out[j : j + 1, :] = top
        stat_out[NY + j : NY + j + 1, :] = jnp.sum(sums[j] * share_of, axis=0, keepdims=True)

    def stat(k):
        return remote(("stat", k), stat_out, stat_in.at[k], at_y(k))

    def delta(k):
        return remote(("delta", k), del_out, del_in.at[k], at_y(k))

    for k in range(1, NY):
        go(stat(k))
    ring_rest(*g_ring)
    for j in (1, 3):
        stack_heads(g_buf[j], gs, j)
    for j in (0, 1, 3):
        slopes(j, 0)
        slopes(j, 1)
    terms = mm_t(rkv_v[:, HEAD:], gs[0])
    dp_own[...] = terms
    products = terms * e_own[...].astype(F32)
    dots[0, 5:6, :] = jnp.sum(fold(products, jnp.sum), axis=0, keepdims=True)
    ring_last(*g_ring)
    stack_heads(g_buf[2], gs, 2)
    for k in range(1, NY):
        stat(k).wait_recv()
    for j in range(NY):
        mine = stat_out[j : j + 1, :]
        others = [stat_in[k, (j + k) % NY : (j + k) % NY + 1, :] for k in range(1, NY)]
        highest = mine
        for other in others:
            highest = jnp.maximum(highest, other)
        factors = [jnp.exp2((top - highest) * EXP2_SCALE) for top in [mine] + others]
        total = stat_out[NY + j : NY + j + 1, :] * factors[0]
        for k in range(1, NY):
            line = NY + (j + k) % NY
            total = total + stat_in[k, line : line + 1, :] * factors[k]
        for k in range(NY):
            row_delta[k, j : j + 1, :] = factors[k] / total
        coef[j] = shares[j] * (factors[0] / total)

    def back(step, c, d):
        sign = -1 if d == 0 else 1
        src, dst, device = {
            2: (s2.at[c, d], q2.at[c, d], at_z(sign)),
            3: (s3.at[c, d], q3.at[c, d], at_z(2 * sign)),
            4: (s4.at[c, pl.ds(2 * d, 2)], q4.at[c, d], at_z(3 * sign)),
            1: (summed.at[c, d], back_in[c][d], at_z(sign)),
        }[step]
        return remote(("back", step, c, d), src, dst, device)

    def fill(c, j, level):
        first, count = levels[level][0] * BLOCK, levels[level][1] * BLOCK
        rows = slice(first, first + count)
        if c == 1:
            p_buf[j, rows, :] = (
                e_buf[j, rows, :].astype(F32) * coef[j, level : level + 1, :]
            ).astype(BF16)
        else:
            ds_buf[j, rows, :] = (
                p_buf[j, rows, :].astype(F32) * (dp_buf[j, rows, :] - row_delta[0, pl.ds(j, 1), :])
            ).astype(BF16)

    def grads(c, j, first, count):
        if c == 1:
            return mm(p_buf[j, first : first + count, :], gs[j])
        return mm(ds_buf[j, first : first + count, :], qs[j]) * SCALE

    def far(c):
        def outer(j):
            fill(c, j, 3)
            terms = grads(c, j, 5 * BLOCK, 3 * BLOCK).astype(BF16)
            s3[c, 0, j] = terms[:BLOCK]
            s3[c, 1, j] = terms[BLOCK : 2 * BLOCK]
            s4[c, j] = terms[2 * BLOCK :]

        def inner(j):
            fill(c, j, 2)
            terms = grads(c, j, 3 * BLOCK, 2 * BLOCK).astype(BF16)
            s2[c, 0, j] = terms[:BLOCK]
            s2[c, 1, j] = terms[BLOCK:]

        each(NY, outer)
        for step in (4, 3):
            for d in range(2):
                go(back(step, c, d))
        each(NY, inner)
        for d in range(2):
            go(back(2, c, d))

    def near(c):
        def one(j):
            for level in range(2):
                fill(c, j, level)
            dkv[c, j] = grads(c, j, 0, 3 * BLOCK)

        each(NY, one)

    def my_terms(c, first, g):
        total = dkv[c, 0, first : first + BLOCK, :] * marks[g]
        for j in range(1, NY):
            total = total + dkv[c, j, first : first + BLOCK, :] * marks[j * GROUPS + g]
        return total

    def add_up(c):
        for d in range(2):
            for step in (4, 3, 2):
                back(step, c, d).wait_recv()

            def one(g):
                total = my_terms(c, (1 + d) * BLOCK, g)
                for i in range(NY):
                    base = NY + 10 * d + i
                    total = total + q2[c, d, i].astype(F32) * marks[base * GROUPS + g]
                    total = total + q3[c, d, i].astype(F32) * marks[(base + 4) * GROUPS + g]
                for i in range(2):
                    total = total + q4[c, d, i].astype(F32) * marks[
                        (NY + 10 * d + 8 + i) * GROUPS + g
                    ]
                summed[c, d, g] = total.astype(BF16)

            each_pair(GROUPS, one)
            go(back(1, c, d))

    def out_copy(c):
        columns = pl.ds(c * HEAD, HEAD)
        return pltpu.make_async_copy(
            op_v.at[c], op_ref.at[0, :, :, columns], out_sem.at[c]
        )

    def finish(c):
        for d in range(2):
            back(1, c, d).wait_recv()
        for slot in range(GROUPS):
            g = pg_ref[0, slot]
            total = back_in[c][0][g].astype(F32) + back_in[c][1][g].astype(F32)
            op_v[c, slot] = (total + my_terms(c, 0, g)).astype(BF16)
        out_copy(c).start()

    far(1)
    slopes(2, 0)
    slopes(2, 1)
    arrived(1, (2,))
    each(NY, lambda j: slopes(j, 2))
    arrived(1, (3, 4))
    each(NY, lambda j: slopes(j, 3))
    for j in range(NY):
        del_out[j : j + 1, :] = jnp.sum(dots[j] * shares[j], axis=0, keepdims=True)
    for k in range(1, NY):
        go(delta(k))
    near(1)
    for k in range(1, NY):
        delta(k).wait_recv()
    for j in range(NY):
        total = del_out[j : j + 1, :] * row_delta[0, j : j + 1, :]
        for k in range(1, NY):
            line = (j + k) % NY
            total = total + del_in[k, line : line + 1, :] * row_delta[k, j : j + 1, :]
        row_delta[0, j : j + 1, :] = total
    far(0)
    listed = list(my_groups)
    for d, sign in ((0, 1), (1, -1)):
        listed += groups[sign] + groups[2 * sign] + groups[3 * sign][2 * d : 2 * d + 2]
    for n, group in enumerate(listed):
        for g in range(GROUPS):
            marks[n * GROUPS + g] = jnp.where(group == g, 1.0, 0.0).astype(F32)
    near(0)
    p_own[...] = (e_own[...].astype(F32) * coef[0, 5:6, :]).astype(BF16)
    ds_own[...] = (
        p_own[...].astype(F32) * (dp_own[...] - row_delta[0, 0:1, :])
    ).astype(BF16)

    def dq_copy(j):
        return remote(("dq", j), dq_send.at[j], dq_recv.at[j], at_y(j))

    for j in range(1, NY):
        dq_send[j] = mm(kv[0, j].T, ds_buf[j]).astype(BF16)
        go(dq_copy(j))
    add_up(1)
    or_v[:, :HEAD] = (mm(ds_own[...], qs[0]) * SCALE).astype(BF16)
    or_v[:, HEAD:] = mm(p_own[...], gs[0]).astype(BF16)
    or_copy = pltpu.make_async_copy(or_v, or_ref, out_sem.at[2])
    or_copy.start()
    dq = mm(kv[0, 0].T, ds_buf[0]) + mm(rkv_v[:, :HEAD].T, ds_own[...])
    add_up(0)
    for j in range(1, NY):
        dq_copy(j).wait_recv()
        dq = dq + dq_recv[j].astype(F32)
    dq = dq * SCALE
    for h in range(HEADS):
        oq_v[:, h * HEAD : (h + 1) * HEAD] = dq[:, h * HEAD : (h + 1) * HEAD].T.astype(BF16)
    oq_copy = pltpu.make_async_copy(oq_v, oq_ref, out_sem.at[3])
    oq_copy.start()
    finish(1)
    for copy in started:
        copy.wait_send()
    finish(0)
    or_copy.wait()
    oq_copy.wait()
    out_copy(1).wait()
    out_copy(0).wait()


def hand_on(*refs):
    sources, targets, held, sem = refs[:3], refs[3:6], refs[6:9], refs[9]
    reads = [pltpu.make_async_copy(sources[n], held[n], sem.at[0, n]) for n in range(3)]
    writes = [pltpu.make_async_copy(held[n], targets[n], sem.at[1, n]) for n in range(3)]
    for copy in reads:
        copy.start()
    for read, write in zip(reads, writes):
        read.wait()
        write.start()
    for copy in writes:
        copy.wait()


def body(
    queries, response_key_value, prompt_kv, prompt_group, response_order, live_blocks,
    out_weight, grad_out,
):
    hbm = pl.BlockSpec(memory_space=pl.ANY)
    smem = pl.BlockSpec(memory_space=pltpu.SMEM)
    block = (BLOCK, HEAD)
    square = (WIDTH, WIDTH)

    def space(*shape, kind=BF16):
        return pltpu.VMEM(shape, kind)

    def streams():
        return [[space(GROUPS, *block) for _ in range(2)] for _ in range(2)]

    scratch = [
        space(*queries.shape),
        space(*response_key_value.shape),
        space(*prompt_kv.shape),
        space(*grad_out.shape),
        space(*queries.shape),
        space(*response_key_value.shape),
        space(2, GROUPS, *block),
        space(PIECES, *square),
        space(NX, TOKENS, WIDTH),
        space(NX, TOKENS, WIDTH),
        space(TOKENS, WIDTH),
        space(NY, TOKENS, WIDTH),
        space(NY, TOKENS, WIDTH),
        space(NY, WIDTH, HEAD),
        space(NY, WIDTH, HEAD),
        space(2, GROUPS, *block),
        streams(),
        space(2, 2, NY, *block),
        space(2, 2, NY, *block),
        space(2, 2, 2, *block),
        space(2, NY, KEYS, HEAD),
        space(NY, KEYS, WIDTH),
        space(TOKENS, WIDTH),
        space(NY, KEYS, WIDTH),
        space(TOKENS, WIDTH),
        space(NY, KEYS, WIDTH, kind=F32),
        space(TOKENS, WIDTH, kind=F32),
        space(NY, KEYS, WIDTH),
        space(TOKENS, WIDTH),
        space(NY, 8, WIDTH, kind=F32),
        space(NY, 8, WIDTH, kind=F32),
        space(NY, 8, WIDTH, kind=F32),
        space(NY, 8, WIDTH, kind=F32),
        space(NY, 8, WIDTH, kind=F32),
        space(NY, 8, WIDTH, kind=F32),
        space(8, WIDTH, kind=F32),
        space(NY, 8, WIDTH, kind=F32),
        space(8, WIDTH, kind=F32),
        space(NY, 8, WIDTH, kind=F32),
        space(2, 2, NY, *block),
        space(2, 2, NY, *block),
        space(2, NY, *block),
        space(2, 2, NY, *block),
        space(2, 2, NY, *block),
        space(2, 2, 2, *block),
        space(2, 2, GROUPS, *block),
        streams(),
        space(2, NY, 3 * BLOCK, HEAD, kind=F32),
        space(NY, HEAD, WIDTH),
        space(NY, HEAD, WIDTH),
        pltpu.SMEM(((NY + 20) * GROUPS,), F32),
        pltpu.SemaphoreType.DMA((4,)),
        pltpu.SemaphoreType.DMA((4,)),
        pltpu.SemaphoreType.DMA((PIECES,)),
        pltpu.SemaphoreType.DMA((N_COPIES,)),
        pltpu.SemaphoreType.DMA((N_COPIES,)),
    ]
    kinds = tuple(
        jax.ShapeDtypeStruct(a.shape, BF16) for a in (queries, response_key_value, prompt_kv)
    )
    outs = pl.pallas_call(
        kernel,
        out_shape=kinds,
        in_specs=[hbm, hbm, hbm, smem, smem, smem, hbm, hbm],
        out_specs=(hbm, hbm, hbm),
        scratch_shapes=scratch,
        compiler_params=pltpu.CompilerParams(
            collective_id=0, has_side_effects=True, vmem_limit_bytes=56 * 1024 * 1024
        ),
        cost_estimate=pl.CostEstimate(
            flops=3_000_000_000, bytes_accessed=8_000_000, transcendentals=1_400_000
        ),
    )(
        queries, response_key_value, prompt_kv, prompt_group, response_order, live_blocks,
        out_weight, grad_out,
    )
    return pl.pallas_call(
        hand_on,
        out_shape=kinds,
        in_specs=[hbm, hbm, hbm],
        out_specs=(hbm, hbm, hbm),
        scratch_shapes=[pltpu.VMEM(a.shape, BF16) for a in kinds]
        + [pltpu.SemaphoreType.DMA((2, 3))],
        compiler_params=pltpu.CompilerParams(vmem_limit_bytes=56 * 1024 * 1024),
    )(*outs)


def solution(mesh):
    return jax.shard_map(
        body,
        mesh=mesh,
        in_specs=(
            P("dp", "tensor"),
            P("dp", "tensor"),
            P("dp", None, None, "tensor"),
            P("dp", None),
            P(),
            P("dp"),
            P("tensor", None),
            P("dp", "tensor"),
        ),
        out_specs=(P("dp", "tensor"), P("dp", "tensor"), P("dp", None, None, "tensor")),
        check_vma=False,
    )
```

time: 240 us -> 58.9 us (0.25)
  waiting for transfers between devices: 126 us -> 0 us
  Pallas kernels: 0 us -> 56.9 us
  blocking collectives: 42 us -> 0 us
  matrix products: 24.2 us -> 0 us
  local copies, waits for them, and re-layouts: 21.8 us -> 0 us
  between operations: 14.9 us -> 1.29 us
  starting transfers between devices: 6.15 us -> 0 us
  other arithmetic: 4.41 us -> 0 us
    all_gather x2 -> x0, waiting for transfers between devices: 79.2 us -> none  [the longest x1 79.2 us: body(): lax.all_gather(prompt_kv, 'dp', axis=0, tiled=True)]
    pallas_call x0 -> x2, Pallas kernels: none -> 56.9 us  [the longest x1 55.1 us: body(): pl.pallas_call(kernel, out_shape=kinds, in_specs=[hbm, hbm, hbm, smem, sm...]
    all_to_all x1 -> x0, waiting for transfers between devices: 45.4 us -> none  [body(): lax.all_to_all(prompt_terms, 'dp', split_axis=0, concat_axis=0, tiled=True)]
    all_gather x1 -> x0, blocking collectives: 42 us -> none  [body(): lax.all_gather(prompt_group, 'dp', axis=0, tiled=True)]
    dot_general x15 -> x0, matrix products: 24.2 us -> none  [the longest x1 5.69 us: body(): jnp.einsum('sc,scx->sx', selector, every_block.reshape(dev_count, groups,...]
    reshape x2 -> x0, local copies, waits for them, and re-layouts: 14 us -> none  [the longest x1 13.5 us: body(): every_block.reshape(dev_count, groups, block_rows * key_value_width)]
    all_to_all x1 -> x0, starting transfers between devices: 6.07 us -> none  [body(): lax.all_to_all(prompt_terms, 'dp', split_axis=0, concat_axis=0, tiled=True)]
    unnamed x12 -> x0, local copies, waits for them, and re-layouts: 3.41 us -> none
  transfers between devices with their start and end apart: 3 -> 0, of which waited for: 2 -> 0; matrix products, arithmetic and copies ran while one was open for 6% -> 0% of each run, Pallas kernels for 0% -> 0%
where the time goes in v1:
time: 58.9 us; the launch traced here: 58.2 us
  Pallas kernels  56.9 us (97%)
  between operations  1.29 us (2%)
    pallas_call x1, Pallas kernels, body(): pl.pallas_call(kernel, out_shape=kinds, in_specs=[hbm, hbm, hbm, smem, sm...  55.1 us
    pallas_call x1, Pallas kernels, body(): pl.pallas_call(hand_on, out_shape=kinds, in_specs=[hbm, hbm, hbm], out_sp...  1.82 us

profile of v1, /device:TPU:2, one launch (start us, length us, event | category | flops | bytes accessed | tf_op | source)
XLA Modules:
  0.0 58.2 jit_solution(10483923415660445739)
XLA Ops:
  1.3 55.1 %shard_map.103 = (bf16[128,640]{1,0:T(8,128)(2,1)}, bf16[128,256]{1,0:T(8,128)(2,1)}, bf16[1,8,64,256]{3,2,1,0:T(8,128)(2,1)}) custom-call(bf16[128,640]{1,0:T(8,128)(2,1)} %q_ref.1, bf16[128,256]{1,0:T(8,128)(2,1)} %rkv_ref.1, bf16[1,8,64,256]{3,2,1,0:T(8,128)(2,1)} %pkv_ref.1, s32[1,8]{1,0:T(1,128)} %pg_ref.1, s32[32]{0:T(128)} %ro_ref.1, ...), custom_call_target="tpu_custom_call" | custom-call | flops 3000000000 | bytes 8000000 | tf_op jit(solution)/shard_map/pallas_call | solution.py:612
  56.4 1.8 %shard_map.104 = (bf16[128,640]{1,0:T(8,128)(2,1)}, bf16[128,256]{1,0:T(8,128)(2,1)}, bf16[1,8,64,256]{3,2,1,0:T(8,128)(2,1)}) custom-call(bf16[128,640]{1,0:T(8,128)(2,1)} %get-tuple-element.6.refs_0_, bf16[128,256]{1,0:T(8,128)(2,1)} %get-tuple-element.7.refs_1_, bf16[1,8,64,256]{3,2,1,0:T(8,128)(2,1)} %get-tuple-element.8.refs_2_), custom_call_target="tpu_custom_call" | custom-call | tf_op jit(solution)/shard_map/pallas_call | solution.py:628

commit v2 on v1

--- a/solution.py
+++ b/solution.py
@@ -54,13 +54,13 @@
 def kernel(
     q_ref, rkv_ref, pkv_ref, pg_ref, ro_ref, lb_ref, w_ref, go_ref,
     oq_ref, or_ref, op_ref,
-    q_v, rkv_v, pkv_v, go_v, oq_v, or_v, op_v,
+    q_v, rkv_v, pkv_v, go_v,
     w_v, gox, gos, g_own, q_buf, g_buf, qs, gs,
     own, r1, st2, st3, st4, kv,
     e_buf, e_own, p_buf, p_own, dp_buf, dp_own, ds_buf, ds_own,
     tops, sums, dots, coef, shares, row_delta, stat_out, stat_in, del_out, del_in,
     s2, s3, s4, q2, q3, q4, summed, back_in, dkv, dq_send, dq_recv,
-    marks, in_sem, out_sem, w_sem, send_sem, recv_sem,
+    marks, in_sem, w_sem, send_sem, recv_sem,
 ):
     dp = lax.axis_index("dp")
     tensor = lax.axis_index("tensor")
@@ -186,7 +186,6 @@
     for d in range(2):
         go(hop(1, 0, d))
     go(share(0))
-    ring_first(*q_ring)
 
     groups = {
         step: [ro_ref[((y + j) % NY) * NZ + (z + step + NZ) % NZ] // 4 for j in range(NY)]
@@ -275,7 +274,7 @@
     go(share(1))
     go(share(3))
     relay(0)
-    ring_second(*q_ring)
+    ring_first(*q_ring)
     grad = grad + project(2, gox.at[1])
     grad = grad + project(6, gox.at[3])
     ring_last(*x_ring)
@@ -285,6 +284,7 @@
     share(3).wait_recv()
     grad = grad + project(7, gos.at[3])
     relay(1)
+    ring_second(*q_ring)
     grad = grad + project(4, gox.at[2])
     share(2).wait_recv()
     grad = grad + project(5, gos.at[2])
@@ -441,20 +441,15 @@
             each_pair(GROUPS, one)
             go(back(1, c, d))
 
-    def out_copy(c):
-        columns = pl.ds(c * HEAD, HEAD)
-        return pltpu.make_async_copy(
-            op_v.at[c], op_ref.at[0, :, :, columns], out_sem.at[c]
-        )
-
     def finish(c):
         for d in range(2):
             back(1, c, d).wait_recv()
         for slot in range(GROUPS):
             g = pg_ref[0, slot]
             total = back_in[c][0][g].astype(F32) + back_in[c][1][g].astype(F32)
-            op_v[c, slot] = (total + my_terms(c, 0, g)).astype(BF16)
-        out_copy(c).start()
+            op_ref[0, slot, :, c * HEAD : (c + 1) * HEAD] = (
+                total + my_terms(c, 0, g)
+            ).astype(BF16)
 
     far(1)
     slopes(2, 0)
@@ -496,10 +491,8 @@
         dq_send[j] = mm(kv[0, j].T, ds_buf[j]).astype(BF16)
         go(dq_copy(j))
     add_up(1)
-    or_v[:, :HEAD] = (mm(ds_own[...], qs[0]) * SCALE).astype(BF16)
-    or_v[:, HEAD:] = mm(p_own[...], gs[0]).astype(BF16)
-    or_copy = pltpu.make_async_copy(or_v, or_ref, out_sem.at[2])
-    or_copy.start()
+    or_ref[:, :HEAD] = (mm(ds_own[...], qs[0]) * SCALE).astype(BF16)
+    or_ref[:, HEAD:] = mm(p_own[...], gs[0]).astype(BF16)
     dq = mm(kv[0, 0].T, ds_buf[0]) + mm(rkv_v[:, :HEAD].T, ds_own[...])
     add_up(0)
     for j in range(1, NY):
@@ -507,29 +500,19 @@
         dq = dq + dq_recv[j].astype(F32)
     dq = dq * SCALE
     for h in range(HEADS):
-        oq_v[:, h * HEAD : (h + 1) * HEAD] = dq[:, h * HEAD : (h + 1) * HEAD].T.astype(BF16)
-    oq_copy = pltpu.make_async_copy(oq_v, oq_ref, out_sem.at[3])
-    oq_copy.start()
+        oq_ref[:, h * HEAD : (h + 1) * HEAD] = dq[:, h * HEAD : (h + 1) * HEAD].T.astype(BF16)
     finish(1)
     for copy in started:
         copy.wait_send()
     finish(0)
-    or_copy.wait()
-    oq_copy.wait()
-    out_copy(1).wait()
-    out_copy(0).wait()
 
 
 def hand_on(*refs):
-    sources, targets, held, sem = refs[:3], refs[3:6], refs[6:9], refs[9]
-    reads = [pltpu.make_async_copy(sources[n], held[n], sem.at[0, n]) for n in range(3)]
-    writes = [pltpu.make_async_copy(held[n], targets[n], sem.at[1, n]) for n in range(3)]
-    for copy in reads:
+    sem = refs[6]
+    copies = [pltpu.make_async_copy(refs[n], refs[3 + n], sem.at[n]) for n in range(3)]
+    for copy in copies:
         copy.start()
-    for read, write in zip(reads, writes):
-        read.wait()
-        write.start()
-    for copy in writes:
+    for copy in copies:
         copy.wait()
 
 
@@ -538,6 +521,7 @@
     out_weight, grad_out,
 ):
     hbm = pl.BlockSpec(memory_space=pl.ANY)
+    vmem = pl.BlockSpec(memory_space=pltpu.VMEM)
     smem = pl.BlockSpec(memory_space=pltpu.SMEM)
     block = (BLOCK, HEAD)
     square = (WIDTH, WIDTH)
@@ -553,9 +537,6 @@
         space(*response_key_value.shape),
         space(*prompt_kv.shape),
         space(*grad_out.shape),
-        space(*queries.shape),
-        space(*response_key_value.shape),
-        space(2, GROUPS, *block),
         space(PIECES, *square),
         space(NX, TOKENS, WIDTH),
         space(NX, TOKENS, WIDTH),
@@ -601,7 +582,6 @@
         space(NY, HEAD, WIDTH),
         pltpu.SMEM(((NY + 20) * GROUPS,), F32),
         pltpu.SemaphoreType.DMA((4,)),
-        pltpu.SemaphoreType.DMA((4,)),
         pltpu.SemaphoreType.DMA((PIECES,)),
         pltpu.SemaphoreType.DMA((N_COPIES,)),
         pltpu.SemaphoreType.DMA((N_COPIES,)),
@@ -611,9 +591,9 @@
     )
     outs = pl.pallas_call(
         kernel,
-        out_shape=kinds,
+        out_shape=tuple(pltpu.VMEM(a.shape, BF16) for a in kinds),
         in_specs=[hbm, hbm, hbm, smem, smem, smem, hbm, hbm],
-        out_specs=(hbm, hbm, hbm),
+        out_specs=(vmem, vmem, vmem),
         scratch_shapes=scratch,
         compiler_params=pltpu.CompilerParams(
             collective_id=0, has_side_effects=True, vmem_limit_bytes=56 * 1024 * 1024
@@ -628,11 +608,9 @@
     return pl.pallas_call(
         hand_on,
         out_shape=kinds,
-        in_specs=[hbm, hbm, hbm],
+        in_specs=[vmem, vmem, vmem],
         out_specs=(hbm, hbm, hbm),
-        scratch_shapes=[pltpu.VMEM(a.shape, BF16) for a in kinds]
-        + [pltpu.SemaphoreType.DMA((2, 3))],
-        compiler_params=pltpu.CompilerParams(vmem_limit_bytes=56 * 1024 * 1024),
+        scratch_shapes=[pltpu.SemaphoreType.DMA((3,))],
     )(*outs)
 
 

time: 58.9 us -> 60.2 us (1.022)
  local copies, waits for them, and re-layouts: 0 us -> 1.95 us
    unnamed x0 -> x6, local copies, waits for them, and re-layouts: none -> 1.95 us
where the time goes in v2:
time: 60.2 us; the launch traced here: 59.8 us
  Pallas kernels  56.5 us (94%)
  local copies, waits for them, and re-layouts  1.95 us (3%)
  between operations  1.3 us (2%)
    pallas_call x1, Pallas kernels, body(): pl.pallas_call(kernel, out_shape=tuple((pltpu.VMEM(a.shape, BF16) for a i...  54.7 us
    unnamed x6, local copies, waits for them, and re-layouts  1.95 us
    pallas_call x1, Pallas kernels, body(): pl.pallas_call(hand_on, out_shape=kinds, in_specs=[vmem, vmem, vmem], out...  1.87 us

profile of v2, /device:TPU:2, one launch (start us, length us, event | category | flops | bytes accessed | tf_op | source)
XLA Modules:
  0.0 59.8 jit_solution(1167537543041796070)
XLA Ops:
  1.3 54.7 %shard_map.103 = (bf16[128,640]{1,0:T(8,128)(2,1)S(1)}, bf16[128,256]{1,0:T(8,128)(2,1)S(1)}, bf16[1,8,64,256]{3,2,1,0:T(8,128)(2,1)S(1)}) custom-call(bf16[128,640]{1,0:T(8,128)(2,1)} %q_ref.1, bf16[128,256]{1,0:T(8,128)(2,1)} %rkv_ref.1, bf16[1,8,64,256]{3,2,1,0:T(8,128)(2,1)} %pkv_ref.1, s32[1,8]{1,0:T(1,128)} %pg_ref.1, s32[32]{0:T(128)} %ro_ref.1, ...), custom_call_target="tpu_custom_call" | custom-call | flops 3000000000 | bytes 8000000 | tf_op jit(solution)/shard_map/pallas_call | solution.py:592
  56.0 0.0 copy-start
  56.0 0.7 %copy-done = bf16[1,8,64,256]{3,2,1,0:T(8,128)(2,1)} copy-done((bf16[1,8,64,256]{3,2,1,0:T(8,128)(2,1)}, bf16[1,8,64,256]{3,2,1,0:T(8,128)(2,1)S(1)}, u32[]{:S(2)}) %copy-start) | copy-done | bytes 262168
  56.6 0.0 copy-start.1
  56.7 0.7 %copy-done.1 = bf16[128,640]{1,0:T(8,128)(2,1)} copy-done((bf16[128,640]{1,0:T(8,128)(2,1)}, bf16[128,640]{1,0:T(8,128)(2,1)S(1)}, u32[]{:S(2)}) %copy-start.1) | copy-done | bytes 163864
  57.3 0.0 copy-start.2
  57.3 0.6 %copy-done.2 = bf16[128,256]{1,0:T(8,128)(2,1)} copy-done((bf16[128,256]{1,0:T(8,128)(2,1)}, bf16[128,256]{1,0:T(8,128)(2,1)S(1)}, u32[]{:S(2)}) %copy-start.2) | copy-done | bytes 65560
  57.9 1.9 %shard_map.104 = (bf16[128,640]{1,0:T(8,128)(2,1)}, bf16[128,256]{1,0:T(8,128)(2,1)}, bf16[1,8,64,256]{3,2,1,0:T(8,128)(2,1)}) custom-call(bf16[128,640]{1,0:T(8,128)(2,1)} %copy-done.1, bf16[128,256]{1,0:T(8,128)(2,1)} %copy-done.2, bf16[1,8,64,256]{3,2,1,0:T(8,128)(2,1)} %copy-done), custom_call_target="tpu_custom_call" | custom-call | tf_op jit(solution)/shard_map/pallas_call | solution.py:608
Async XLA Ops:
  56.0 0.7 %copy-start = (bf16[1,8,64,256]{3,2,1,0:T(8,128)(2,1)}, bf16[1,8,64,256]{3,2,1,0:T(8,128)(2,1)S(1)}, u32[]{:S(2)}) copy-start(bf16[1,8,64,256]{3,2,1,0:T(8,128)(2,1)S(1)} %get-tuple-element.8.refs_2_) | copy-start | bytes 786436
  56.6 0.7 %copy-start.1 = (bf16[128,640]{1,0:T(8,128)(2,1)}, bf16[128,640]{1,0:T(8,128)(2,1)S(1)}, u32[]{:S(2)}) copy-start(bf16[128,640]{1,0:T(8,128)(2,1)S(1)} %get-tuple-element.6.refs_0_) | copy-start | bytes 491524
  57.3 0.6 %copy-start.2 = (bf16[128,256]{1,0:T(8,128)(2,1)}, bf16[128,256]{1,0:T(8,128)(2,1)S(1)}, u32[]{:S(2)}) copy-start(bf16[128,256]{1,0:T(8,128)(2,1)S(1)} %get-tuple-element.7.refs_1_) | copy-start | bytes 196612

commit v3 on v2

v3 whole, which is shorter than its diff:
```python
import math

import jax
import jax.numpy as jnp
from jax import lax
from jax.experimental import pallas as pl
from jax.experimental.pallas import tpu as pltpu
from jax.sharding import PartitionSpec as P

HEAD = 128
HEADS = 5
WIDTH = HEAD * HEADS
TOKENS = 128
BLOCK = 64
GROUPS = 8
NY, NZ, NX = 4, 8, 4
PIECES = 8
PROMPT = NZ * NY * BLOCK
SLOT = NY * BLOCK
SCALE = 1.0 / math.sqrt(HEAD)
EXP2_SCALE = SCALE * math.log2(math.e)
N_COPIES = 150
MESH = pl.DeviceIdType.MESH
BF16, F32 = jnp.bfloat16, jnp.float32

def mm(a, b):
    return jnp.dot(a, b, preferred_element_type=F32)


def mm_t(a, b):
    return lax.dot_general(a, b, (((1,), (1,)), ((), ())), preferred_element_type=F32)


def fold(x, op):
    return op(x.reshape(x.shape[0] // 8, 8, x.shape[1]), axis=0)


def each(count, step):
    def run(index, carry):
        step(index)
        return carry

    lax.fori_loop(0, count, run, 0)


def each_pair(count, step):
    def both(index):
        step(2 * index)
        step(2 * index + 1)

    each(count // 2, both)


LEVELS = [(0,), (1, 2), (3, 4), (5, 6, 7)]
LAST = 8


def kernel(
    q_ref, rkv_ref, pkv_ref, pg_ref, ro_ref, lb_ref, w_ref, go_ref,
    oq_ref, or_ref, op_ref,
    q_v, pkv_v, go_v,
    w_v, gox, gos, qs, gs,
    own, r1, picked, picked_own, kv,
    e_buf, p_buf, dp_buf, ds_buf,
    tops, sums, dots, coef, row_delta,
    terms, relayed, direct, summed, back_in,
    marks, in_sem, w_sem, send_sem, recv_sem,
):
    dp = lax.axis_index("dp")
    tensor = lax.axis_index("tensor")
    y, z = dp // NZ, dp % NZ
    x, core = tensor // 2, tensor % 2

    def at(dy, dz):
        return (((y + dy) % NY) * NZ + (z + dz + NZ) % NZ, tensor)

    def at_x(step):
        return (dp, ((x + step + NX) % NX) * 2 + core)

    sibling = (dp, x * 2 + 1 - core)

    numbers = {}
    started = []

    def remote(name, src, dst, device):
        n = numbers.setdefault(name, len(numbers))
        return pltpu.make_async_remote_copy(
            src_ref=src, dst_ref=dst, send_sem=send_sem.at[n], recv_sem=recv_sem.at[n],
            device_id=device, device_id_type=MESH,
        )

    def go(copy):
        copy.start()
        started.append(copy)

    barrier = pltpu.get_barrier_semaphore()
    partners = [at(dy, dz) for dz in range(-3, 4) for dy in range(NY) if (dy, dz) != (0, 0)]
    partners += [at_x(1), at_x(-1), sibling]
    for partner in partners:
        pl.semaphore_signal(barrier, inc=1, device_id=partner, device_id_type=MESH)
    in_copies = [
        pltpu.make_async_copy(src, dst, in_sem.at[n])
        for n, (src, dst) in enumerate(
            [
                (pkv_ref, pkv_v), (go_ref, go_v), (q_ref, q_v),
                (rkv_ref.at[:, pl.ds(0, HEAD)], kv.at[0, pl.ds(PROMPT, TOKENS)]),
                (rkv_ref.at[:, pl.ds(HEAD, HEAD)], kv.at[1, pl.ds(PROMPT, TOKENS)]),
            ]
        )
    ]
    for copy in in_copies:
        copy.start()

    w_copies = []
    for r in range(NX):
        for other in range(2):
            piece = ((x + r) % NX) * 2 + (core if other == 0 else 1 - core)
            copy = pltpu.make_async_copy(
                w_ref.at[:, pl.ds(pl.multiple_of(piece * WIDTH, WIDTH), WIDTH)],
                w_v.at[r * 2 + other], w_sem.at[r * 2 + other],
            )
            copy.start()
            w_copies.append(copy)

    groups = {
        dz: [ro_ref[((y + dy) % NY) * NZ + (z + dz + NZ) % NZ] // 4 for dy in range(NY)]
        for dz in range(-3, 4)
    }

    in_copies[0].wait()
    for g in range(GROUPS):
        slot = jnp.int32(0)
        for c in range(GROUPS):
            slot = jnp.where(pg_ref[0, c] == g, c, slot)
        block = pkv_v[0, slot]
        own[0, g] = block[:, :HEAD]
        own[1, g] = block[:, HEAD:]
    for c in range(2):
        for dy in range(NY):
            if dy == 0:
                kv[c, 0:BLOCK, :] = own[c, groups[0][0]]
            else:
                picked_own[c, dy] = own[c, groups[0][dy]]
    for copy in in_copies[1:]:
        copy.wait()
    pl.semaphore_wait(barrier, len(partners))

    def first_hop(c, d):
        return remote(("first", c, d), own.at[c], r1[c][d], at(0, 1 if d == 0 else -1))

    def place(slot, dy):
        return pl.ds(slot * SLOT + (dy % NY) * BLOCK, BLOCK)

    def own_copy(c, dy):
        return remote(
            ("own", c, dy), picked_own.at[c, dy], kv.at[c, place(0, -dy)], at(dy, 0)
        )

    def forward(c, d, m, dy):
        slot = 7 if m == 3 else 1 + d + 2 * m
        return remote(
            ("forward", c, d, m, dy), picked.at[c, d, m, dy], kv.at[c, place(slot, -dy)],
            at(dy, m if d == 0 else -m),
        )

    def sent(d, m):
        if m == 3:
            return (2 * d, 2 * d + 1)
        return (1, 2, 3) if m == 0 else (0, 1, 2, 3)

    def relay(c):
        for d in range(2):
            sign = 1 if d == 0 else -1
            first_hop(c, d).wait_recv()
            for m in (3, 2, 1, 0):
                for dy in sent(d, m):
                    picked[c, d, m, dy] = r1[c][d][groups[sign * m][dy]]
                    go(forward(c, d, m, dy))
            kv[c, (1 + d) * SLOT : (1 + d) * SLOT + BLOCK, :] = r1[c][d][groups[0][0]]

    def arrived(c, level):
        if level == 0:
            for dy in range(1, NY):
                own_copy(c, dy).wait_recv()
        else:
            for m in (3, 2) if level == 3 else (level - 1,):
                for d in range(2):
                    for dy in sent(d, m):
                        forward(c, d, m, dy).wait_recv()

    half = TOKENS // 2

    def x_copy(way, part):
        rows = pl.ds(part * half, half)
        return remote(
            ("x", way, part), go_v.at[rows], gox.at[1 if way == 0 else 3, rows],
            at_x(-1 if way == 0 else 1),
        )

    def x_pass(way):
        rows = pl.ds(way * half, half)
        return remote(
            ("x", way, 2), gox.at[1 if way == 0 else 3, rows], gox.at[2, rows],
            at_x(-1 if way == 0 else 1),
        )

    def share(r):
        src = go_v if r == 0 else gox.at[r]
        return remote(("share", r), src, gos.at[r], sibling)

    for way in range(2):
        go(x_copy(way, way))
    for d in range(2):
        go(first_hop(0, d))
    for way in range(2):
        go(x_copy(way, 1 - way))
    go(share(0))
    for dy in range(1, NY):
        go(own_copy(0, dy))

    def rows_of(chunk):
        if isinstance(chunk, int) and chunk == LAST:
            return pl.ds(PROMPT, TOKENS)
        return pl.ds(pl.multiple_of(chunk * SLOT, SLOT), SLOT)

    def scores(chunk):
        rows = rows_of(chunk)
        s = mm_t(kv[0, rows, :], qs[...])
        if isinstance(chunk, int) and chunk == LAST:
            key_pos = lax.broadcasted_iota(jnp.int32, s.shape, 0)
            query_pos = lax.broadcasted_iota(jnp.int32, s.shape, 1) % TOKENS
            s = jnp.where(key_pos <= query_pos, s, -jnp.inf)
        top = jnp.max(fold(s, jnp.max), axis=0, keepdims=True)
        e = jnp.exp2((s - top) * EXP2_SCALE)
        e_buf[rows, :] = e.astype(BF16)
        tops[chunk] = top
        sums[chunk] = jnp.sum(fold(e, jnp.sum), axis=0, keepdims=True)

    def slopes(chunk):
        rows = rows_of(chunk)
        values = mm_t(kv[1, rows, :], gs[...])
        dp_buf[rows, :] = values
        products = values * e_buf[rows, :].astype(F32)
        dots[chunk] = jnp.sum(fold(products, jnp.sum), axis=0, keepdims=True)

    def level_of(number, step):
        slots = LEVELS[number]
        each(len(slots), lambda i: step(slots[0] + i))

    def project(piece, block):
        w_copies[piece].wait()
        return mm_t(w_v[piece], block[...])

    grad = project(0, go_v)
    for d in range(2):
        go(first_hop(1, d))
    for dy in range(1, NY):
        go(own_copy(1, dy))
    for h in range(HEADS):
        qs[h * HEAD : (h + 1) * HEAD, :] = q_v[:, h * HEAD : (h + 1) * HEAD]
    share(0).wait_recv()
    grad = grad + project(1, gos.at[0])
    scores(LAST)
    for way in range(2):
        x_copy(way, way).wait_recv()
        go(x_pass(way))
    relay(0)
    for way in range(2):
        x_copy(way, 1 - way).wait_recv()
    go(share(1))
    go(share(3))
    grad = grad + project(2, gox.at[1])
    grad = grad + project(6, gox.at[3])
    for way in range(2):
        x_pass(way).wait_recv()
    go(share(2))
    share(1).wait_recv()
    grad = grad + project(3, gos.at[1])
    share(3).wait_recv()
    grad = grad + project(7, gos.at[3])
    relay(1)
    grad = grad + project(4, gox.at[2])
    share(2).wait_recv()
    grad = grad + project(5, gos.at[2])
    column = lax.broadcasted_iota(jnp.int32, grad.shape, 1)
    grad = jnp.where(column < lb_ref[0] * TOKENS, grad, 0.0).astype(BF16)
    for h in range(HEADS):
        rows = slice(h * HEAD, (h + 1) * HEAD)
        gs[rows, :] = grad[rows, :].T

    arrived(0, 0)
    level_of(0, scores)
    slopes(LAST)
    arrived(0, 1)
    level_of(1, scores)
    arrived(1, 0)
    level_of(0, slopes)
    arrived(0, 2)
    level_of(2, scores)
    arrived(0, 3)
    level_of(3, scores)

    highest = tops[0]
    for chunk in range(1, LAST + 1):
        highest = jnp.maximum(highest, tops[chunk])
    factors = [jnp.exp2((tops[chunk] - highest) * EXP2_SCALE) for chunk in range(LAST + 1)]
    total = sums[0] * factors[0]
    for chunk in range(1, LAST + 1):
        total = total + sums[chunk] * factors[chunk]
    for chunk in range(LAST + 1):
        coef[chunk] = factors[chunk] / total

    def back(c, slot, dy):
        src = terms.at[c, place(slot, dy)]
        if slot == 0:
            dst, device = direct.at[c, -dy % NY], at(dy, 0)
        else:
            m, d = (3, dy // 2) if slot == 7 else divmod(slot - 1, 2)
            index = 12 + dy % 2 if slot == 7 else m * NY + -dy % NY
            dst, device = relayed.at[c, d, index], at(dy, -m if d == 0 else m)
        return remote(("back", c, slot, dy), src, dst, device)

    def summed_copy(c, d):
        return remote(
            ("summed", c, d), summed.at[c, d], back_in[c][d], at(0, -1 if d == 0 else 1)
        )

    def returned(slot):
        return (1, 2, 3) if slot < 3 else (0, 1, 2, 3)

    def fill(c, chunk):
        rows = rows_of(chunk)
        if c == 1:
            p = e_buf[rows, :].astype(F32) * coef[chunk]
            p_buf[rows, :] = p.astype(BF16)
            return mm(p_buf[rows, :], gs[...])
        ds = p_buf[rows, :].astype(F32) * (dp_buf[rows, :] - row_delta[...])
        ds_buf[rows, :] = ds.astype(BF16)
        return mm(ds_buf[rows, :], qs[...]) * SCALE

    def send_back(c, number):
        def one(chunk):
            terms[c, rows_of(chunk), :] = fill(c, chunk).astype(BF16)

        level_of(number, one)
        for slot in reversed(LEVELS[number]):
            for dy in returned(slot):
                go(back(c, slot, dy))

    def mark(d, i, g):
        return marks[(d * 14 + i) * GROUPS + g]

    def add_up(c):
        for d in range(2):
            for slot in (7, 5 + d, 3 + d, 1 + d):
                for dy in (2 * d, 2 * d + 1) if slot == 7 else returned(slot):
                    back(c, slot, dy).wait_recv()

            def one(g):
                mine = terms[c, (1 + d) * SLOT : (1 + d) * SLOT + BLOCK, :]
                result = mine.astype(F32) * mark(d, 0, g)
                for i in range(1, 14):
                    result = result + relayed[c, d, i].astype(F32) * mark(d, i, g)
                summed[c, d, g] = result.astype(BF16)

            each_pair(GROUPS, one)
            go(summed_copy(c, d))

    def finish(c):
        for dy in returned(0):
            back(c, 0, dy).wait_recv()
        for d in range(2):
            summed_copy(c, d).wait_recv()
        for slot in range(GROUPS):
            g = pg_ref[0, slot]
            result = back_in[c][0][g].astype(F32) + back_in[c][1][g].astype(F32)
            result = result + terms[c, 0:BLOCK, :].astype(F32) * mark(0, 0, g)
            for dy in range(1, NY):
                result = result + direct[c, dy].astype(F32) * mark(0, dy, g)
            op_ref[0, slot, :, c * HEAD : (c + 1) * HEAD] = result.astype(BF16)

    send_back(1, 3)
    send_back(1, 2)
    arrived(1, 1)
    level_of(1, slopes)
    arrived(1, 2)
    level_of(2, slopes)
    arrived(1, 3)
    level_of(3, slopes)
    delta = dots[0] * coef[0]
    for chunk in range(1, LAST + 1):
        delta = delta + dots[chunk] * coef[chunk]
    row_delta[...] = delta
    send_back(0, 3)
    send_back(0, 2)
    send_back(1, 1)
    send_back(1, 0)
    send_back(0, 1)
    send_back(0, 0)
    listed = []
    for d, sign in ((0, 1), (1, -1)):
        for m in range(3):
            listed += groups[sign * m]
        listed += [groups[sign * 3][-dy % NY] for dy in (2 * d, 2 * d + 1)]
    for n, group in enumerate(listed):
        for g in range(GROUPS):
            marks[n * GROUPS + g] = jnp.where(group == g, 1.0, 0.0).astype(F32)
    or_ref[:, HEAD:] = fill(1, LAST).astype(BF16)
    or_ref[:, :HEAD] = fill(0, LAST).astype(BF16)
    add_up(1)
    dq = mm(kv[0].T, ds_buf[...]) * SCALE
    for h in range(HEADS):
        oq_ref[:, h * HEAD : (h + 1) * HEAD] = dq[:, h * HEAD : (h + 1) * HEAD].T.astype(BF16)
    add_up(0)
    finish(1)
    for copy in started:
        copy.wait_send()
    finish(0)


def hand_on(*refs):
    sem = refs[6]
    copies = [pltpu.make_async_copy(refs[n], refs[3 + n], sem.at[n]) for n in range(3)]
    for copy in copies:
        copy.start()
    for copy in copies:
        copy.wait()


def body(
    queries, response_key_value, prompt_kv, prompt_group, response_order, live_blocks,
    out_weight, grad_out,
):
    hbm = pl.BlockSpec(memory_space=pl.ANY)
    vmem = pl.BlockSpec(memory_space=pltpu.VMEM)
    smem = pl.BlockSpec(memory_space=pltpu.SMEM)
    block = (BLOCK, HEAD)
    square = (WIDTH, WIDTH)

    def space(*shape, kind=BF16):
        return pltpu.VMEM(shape, kind)

    def streams():
        return [[space(GROUPS, *block) for _ in range(2)] for _ in range(2)]

    scratch = [
        space(*queries.shape),
        space(*prompt_kv.shape),
        space(*grad_out.shape),
        space(PIECES, *square),
        space(NX, TOKENS, WIDTH),
        space(NX, TOKENS, WIDTH),
        space(WIDTH, HEAD),
        space(WIDTH, HEAD),
        space(2, GROUPS, *block),
        streams(),
        space(2, 2, 4, NY, *block),
        space(2, NY, *block),
        space(2, PROMPT + TOKENS, HEAD),
        space(PROMPT + TOKENS, WIDTH),
        space(PROMPT + TOKENS, WIDTH),
        space(PROMPT + TOKENS, WIDTH, kind=F32),
        space(PROMPT + TOKENS, WIDTH),
        space(LAST + 1, 1, WIDTH, kind=F32),
        space(LAST + 1, 1, WIDTH, kind=F32),
        space(LAST + 1, 1, WIDTH, kind=F32),
        space(LAST + 1, 1, WIDTH, kind=F32),
        space(1, WIDTH, kind=F32),
        space(2, PROMPT, HEAD),
        space(2, 2, 14, *block),
        space(2, NY, *block),
        space(2, 2, GROUPS, *block),
        streams(),
        pltpu.SMEM((28 * GROUPS,), F32),
        pltpu.SemaphoreType.DMA((5,)),
        pltpu.SemaphoreType.DMA((PIECES,)),
        pltpu.SemaphoreType.DMA((N_COPIES,)),
        pltpu.SemaphoreType.DMA((N_COPIES,)),
    ]
    kinds = tuple(
        jax.ShapeDtypeStruct(a.shape, BF16) for a in (queries, response_key_value, prompt_kv)
    )
    outs = pl.pallas_call(
        kernel,
        out_shape=tuple(pltpu.VMEM(a.shape, BF16) for a in kinds),
        in_specs=[hbm, hbm, hbm, smem, smem, smem, hbm, hbm],
        out_specs=(vmem, vmem, vmem),
        scratch_shapes=scratch,
        compiler_params=pltpu.CompilerParams(
            collective_id=0, has_side_effects=True, vmem_limit_bytes=56 * 1024 * 1024
        ),
        cost_estimate=pl.CostEstimate(
            flops=3_000_000_000, bytes_accessed=8_000_000, transcendentals=1_400_000
        ),
    )(
        queries, response_key_value, prompt_kv, prompt_group, response_order, live_blocks,
        out_weight, grad_out,
    )
    outs = [pltpu.with_memory_space_constraint(out, pltpu.VMEM) for out in outs]
    return pl.pallas_call(
        hand_on,
        out_shape=kinds,
        in_specs=[vmem, vmem, vmem],
        out_specs=(hbm, hbm, hbm),
        scratch_shapes=[pltpu.SemaphoreType.DMA((3,))],
        compiler_params=pltpu.CompilerParams(vmem_limit_bytes=1024 * 1024),
    )(*outs)


def solution(mesh):
    return jax.shard_map(
        body,
        mesh=mesh,
        in_specs=(
            P("dp", "tensor"),
            P("dp", "tensor"),
            P("dp", None, None, "tensor"),
            P("dp", None),
            P(),
            P("dp"),
            P("tensor", None),
            P("dp", "tensor"),
        ),
        out_specs=(P("dp", "tensor"), P("dp", "tensor"), P("dp", None, None, "tensor")),
        check_vma=False,
    )
```

time: 60.2 us -> 55.5 us (0.922)
  Pallas kernels: 56.5 us -> 54.1 us
  local copies, waits for them, and re-layouts: 1.95 us -> 0 us
    unnamed x6 -> x0, local copies, waits for them, and re-layouts: 1.95 us -> none
    pallas_call x1, Pallas kernels: 54.7 us -> 53.3 us  [body(): pl.pallas_call(kernel, out_shape=tuple((pltpu.VMEM(a.shape, BF16) for a i...]
    pallas_call x1, Pallas kernels: 1.87 us -> 0.81 us  [body(): pl.pallas_call(hand_on, out_shape=kinds, in_specs=[vmem, vmem, vmem], out...]
where the time goes in v3:
time: 55.5 us; the launch traced here: 55.4 us
  Pallas kernels  54.1 us (97%)
  between operations  1.29 us (2%)
    pallas_call x1, Pallas kernels, body(): pl.pallas_call(kernel, out_shape=tuple((pltpu.VMEM(a.shape, BF16) for a i...  53.3 us

profile of v3, /device:TPU:2, one launch (start us, length us, event | category | flops | bytes accessed | tf_op | source)
XLA Modules:
  0.0 55.4 jit_solution(4851145315609222585)
XLA Ops:
  1.3 53.3 %shard_map.103 = (bf16[128,640]{1,0:T(8,128)(2,1)S(1)}, bf16[128,256]{1,0:T(8,128)(2,1)S(1)}, bf16[1,8,64,256]{3,2,1,0:T(8,128)(2,1)S(1)}) custom-call(bf16[128,640]{1,0:T(8,128)(2,1)} %q_ref.1, bf16[128,256]{1,0:T(8,128)(2,1)} %rkv_ref.1, bf16[1,8,64,256]{3,2,1,0:T(8,128)(2,1)} %pkv_ref.1, s32[1,8]{1,0:T(1,128)} %pg_ref.1, s32[32]{0:T(128)} %ro_ref.1, ...), custom_call_target="tpu_custom_call" | custom-call | flops 3000000000 | bytes 8000000 | tf_op jit(solution)/shard_map/pallas_call | solution.py:483
  54.6 0.8 %shard_map.104 = (bf16[128,640]{1,0:T(8,128)(2,1)}, bf16[128,256]{1,0:T(8,128)(2,1)}, bf16[1,8,64,256]{3,2,1,0:T(8,128)(2,1)}) custom-call(bf16[128,640]{1,0:T(8,128)(2,1)S(1)} %get-tuple-element.6.refs_0_, bf16[128,256]{1,0:T(8,128)(2,1)S(1)} %get-tuple-element.7.refs_1_, bf16[1,8,64,256]{3,2,1,0:T(8,128)(2,1)S(1)} %get-tuple-element.8.refs_2_), custom_call_target="tpu_custom_call" | custom-call | tf_op jit(solution)/shard_map/pallas_call | solution.py:500

commit v4 on v3

--- a/solution.py
+++ b/solution.py
@@ -14,7 +14,6 @@
 BLOCK = 64
 GROUPS = 8
 NY, NZ, NX = 4, 8, 4
-PIECES = 8
 PROMPT = NZ * NY * BLOCK
 SLOT = NY * BLOCK
 SCALE = 1.0 / math.sqrt(HEAD)
@@ -58,24 +57,29 @@
 def kernel(
     q_ref, rkv_ref, pkv_ref, pg_ref, ro_ref, lb_ref, w_ref, go_ref,
     oq_ref, or_ref, op_ref,
-    q_v, pkv_v, go_v,
-    w_v, gox, gos, qs, gs,
+    q_v, pkv_v,
+    w_v, gathered, qs, gs,
     own, r1, picked, picked_own, kv,
     e_buf, p_buf, dp_buf, ds_buf,
     tops, sums, dots, coef, row_delta,
-    terms, relayed, direct, summed, back_in,
+    terms, relayed, direct, summed, back_in, local,
     marks, in_sem, w_sem, send_sem, recv_sem,
 ):
     dp = lax.axis_index("dp")
     tensor = lax.axis_index("tensor")
-    y, z = dp // NZ, dp % NZ
-    x, core = tensor // 2, tensor % 2
+    y, z = lax.div(dp, NZ), lax.rem(dp, NZ)
+    x, core = lax.div(tensor, 2), lax.rem(tensor, 2)
+
+    ys = [lax.rem(y + dy, NY) for dy in range(NY)]
+    zs = {dz: lax.rem(z + dz + NZ, NZ) for dz in range(-3, 4)}
+    places = {(dy, dz): ys[dy] * NZ + zs[dz] for dy in range(NY) for dz in zs}
+    along_x = {step: lax.rem(x + step + NX, NX) * 2 + core for step in (-1, 1)}
 
     def at(dy, dz):
-        return (((y + dy) % NY) * NZ + (z + dz + NZ) % NZ, tensor)
+        return (places[dy, dz], tensor)
 
     def at_x(step):
-        return (dp, ((x + step + NX) % NX) * 2 + core)
+        return (dp, along_x[step])
 
     sibling = (dp, x * 2 + 1 - core)
 
@@ -93,54 +97,34 @@
         copy.start()
         started.append(copy)
 
+    in_copies = [
+        pltpu.make_async_copy(src, dst, in_sem.at[n])
+        for n, (src, dst) in enumerate(
+            [
+                (pkv_ref, pkv_v), (go_ref, gathered.at[0, :, pl.ds(0, WIDTH)]), (q_ref, q_v),
+                (rkv_ref.at[:, pl.ds(0, HEAD)], kv.at[0, pl.ds(PROMPT, TOKENS)]),
+                (rkv_ref.at[:, pl.ds(HEAD, HEAD)], kv.at[1, pl.ds(PROMPT, TOKENS)]),
+            ]
+        )
+    ]
+    in_copies[0].start()
     barrier = pltpu.get_barrier_semaphore()
     partners = [at(dy, dz) for dz in range(-3, 4) for dy in range(NY) if (dy, dz) != (0, 0)]
     partners += [at_x(1), at_x(-1), sibling]
     for partner in partners:
         pl.semaphore_signal(barrier, inc=1, device_id=partner, device_id_type=MESH)
-    in_copies = [
-        pltpu.make_async_copy(src, dst, in_sem.at[n])
-        for n, (src, dst) in enumerate(
-            [
-                (pkv_ref, pkv_v), (go_ref, go_v), (q_ref, q_v),
-                (rkv_ref.at[:, pl.ds(0, HEAD)], kv.at[0, pl.ds(PROMPT, TOKENS)]),
-                (rkv_ref.at[:, pl.ds(HEAD, HEAD)], kv.at[1, pl.ds(PROMPT, TOKENS)]),
-            ]
-        )
-    ]
-    for copy in in_copies:
+    for copy in in_copies[1:]:
         copy.start()
 
-    w_copies = []
-    for r in range(NX):
-        for other in range(2):
-            piece = ((x + r) % NX) * 2 + (core if other == 0 else 1 - core)
-            copy = pltpu.make_async_copy(
-                w_ref.at[:, pl.ds(pl.multiple_of(piece * WIDTH, WIDTH), WIDTH)],
-                w_v.at[r * 2 + other], w_sem.at[r * 2 + other],
-            )
-            copy.start()
-            w_copies.append(copy)
-
-    groups = {
-        dz: [ro_ref[((y + dy) % NY) * NZ + (z + dz + NZ) % NZ] // 4 for dy in range(NY)]
-        for dz in range(-3, 4)
-    }
-
-    in_copies[0].wait()
+    slot_of = []
     for g in range(GROUPS):
         slot = jnp.int32(0)
         for c in range(GROUPS):
             slot = jnp.where(pg_ref[0, c] == g, c, slot)
-        block = pkv_v[0, slot]
-        own[0, g] = block[:, :HEAD]
-        own[1, g] = block[:, HEAD:]
-    for c in range(2):
-        for dy in range(NY):
-            if dy == 0:
-                kv[c, 0:BLOCK, :] = own[c, groups[0][0]]
-            else:
-                picked_own[c, dy] = own[c, groups[0][dy]]
+        slot_of.append(slot)
+    in_copies[0].wait()
+    for g in range(GROUPS):
+        own[0, g] = pkv_v[0, slot_of[g], :, :HEAD]
     for copy in in_copies[1:]:
         copy.wait()
     pl.semaphore_wait(barrier, len(partners))
@@ -151,9 +135,9 @@
     def place(slot, dy):
         return pl.ds(slot * SLOT + (dy % NY) * BLOCK, BLOCK)
 
-    def own_copy(c, dy):
+    def own_copy(dy):
         return remote(
-            ("own", c, dy), picked_own.at[c, dy], kv.at[c, place(0, -dy)], at(dy, 0)
+            ("own", dy), picked_own.at[:, dy], kv.at[:, place(0, -dy)], at(dy, 0)
         )
 
     def forward(c, d, m, dy):
@@ -181,7 +165,7 @@
     def arrived(c, level):
         if level == 0:
             for dy in range(1, NY):
-                own_copy(c, dy).wait_recv()
+                own_copy(dy).wait_recv()
         else:
             for m in (3, 2) if level == 3 else (level - 1,):
                 for d in range(2):
@@ -190,33 +174,59 @@
 
     half = TOKENS // 2
 
+    def slice_of(r, other, rows=pl.ds(0, TOKENS)):
+        return gathered.at[r, rows, pl.ds(other * WIDTH, WIDTH)]
+
     def x_copy(way, part):
         rows = pl.ds(part * half, half)
         return remote(
-            ("x", way, part), go_v.at[rows], gox.at[1 if way == 0 else 3, rows],
+            ("x", way, part), slice_of(0, 0, rows), slice_of(1 if way == 0 else 3, 0, rows),
             at_x(-1 if way == 0 else 1),
         )
 
     def x_pass(way):
         rows = pl.ds(way * half, half)
         return remote(
-            ("x", way, 2), gox.at[1 if way == 0 else 3, rows], gox.at[2, rows],
+            ("x", way, 2), slice_of(1 if way == 0 else 3, 0, rows), slice_of(2, 0, rows),
             at_x(-1 if way == 0 else 1),
         )
 
     def share(r):
-        src = go_v if r == 0 else gox.at[r]
-        return remote(("share", r), src, gos.at[r], sibling)
-
-    for way in range(2):
-        go(x_copy(way, way))
+        return remote(("share", r), slice_of(r, 0), slice_of(r, 1), sibling)
+
     for d in range(2):
         go(first_hop(0, d))
-    for way in range(2):
-        go(x_copy(way, 1 - way))
+    for part in range(2):
+        for way in range(2):
+            go(x_copy(way, way if part == 0 else 1 - way))
     go(share(0))
-    for dy in range(1, NY):
-        go(own_copy(0, dy))
+
+    w_copies = {}
+    for r in (0, 1, 3, 2):
+        for other in range(2):
+            piece = lax.rem(x + r, NX) * 2 + (core if other == 0 else 1 - core)
+            copy = pltpu.make_async_copy(
+                w_ref.at[:, pl.ds(pl.multiple_of(piece * WIDTH, WIDTH), WIDTH)],
+                w_v.at[r, :, pl.ds(other * WIDTH, WIDTH)], w_sem.at[r, other],
+            )
+            copy.start()
+            w_copies[r, other] = copy
+    for g in range(GROUPS):
+        own[1, g] = pkv_v[0, slot_of[g], :, HEAD:]
+    for d in range(2):
+        go(first_hop(1, d))
+
+    groups = {
+        dz: [lax.div(ro_ref[places[dy, dz]], 4) for dy in range(NY)] for dz in range(-3, 4)
+    }
+    for dy in range(NY):
+        for c in range(2):
+            if dy == 0:
+                kv[c, 0:BLOCK, :] = own[c, groups[0][0]]
+            else:
+                picked_own[c, dy] = own[c, groups[0][dy]]
+        if dy > 0:
+            go(own_copy(dy))
 
     def rows_of(chunk):
         if isinstance(chunk, int) and chunk == LAST:
@@ -247,54 +257,45 @@
         slots = LEVELS[number]
         each(len(slots), lambda i: step(slots[0] + i))
 
-    def project(piece, block):
-        w_copies[piece].wait()
-        return mm_t(w_v[piece], block[...])
-
-    grad = project(0, go_v)
-    for d in range(2):
-        go(first_hop(1, d))
-    for dy in range(1, NY):
-        go(own_copy(1, dy))
+    def project(r):
+        for other in range(2):
+            w_copies[r, other].wait()
+        return mm_t(w_v[r], gathered[r])
+
     for h in range(HEADS):
         qs[h * HEAD : (h + 1) * HEAD, :] = q_v[:, h * HEAD : (h + 1) * HEAD]
+    scores(LAST)
     share(0).wait_recv()
-    grad = grad + project(1, gos.at[0])
-    scores(LAST)
+    grad = project(0)
     for way in range(2):
         x_copy(way, way).wait_recv()
         go(x_pass(way))
     relay(0)
     for way in range(2):
         x_copy(way, 1 - way).wait_recv()
-    go(share(1))
-    go(share(3))
-    grad = grad + project(2, gox.at[1])
-    grad = grad + project(6, gox.at[3])
+        go(share(1 if way == 0 else 3))
+    arrived(0, 0)
+    level_of(0, scores)
     for way in range(2):
         x_pass(way).wait_recv()
     go(share(2))
     share(1).wait_recv()
-    grad = grad + project(3, gos.at[1])
+    grad = grad + project(1)
+    relay(1)
     share(3).wait_recv()
-    grad = grad + project(7, gos.at[3])
-    relay(1)
-    grad = grad + project(4, gox.at[2])
+    grad = grad + project(3)
     share(2).wait_recv()
-    grad = grad + project(5, gos.at[2])
+    grad = grad + project(2)
     column = lax.broadcasted_iota(jnp.int32, grad.shape, 1)
     grad = jnp.where(column < lb_ref[0] * TOKENS, grad, 0.0).astype(BF16)
     for h in range(HEADS):
         rows = slice(h * HEAD, (h + 1) * HEAD)
         gs[rows, :] = grad[rows, :].T
 
-    arrived(0, 0)
-    level_of(0, scores)
     slopes(LAST)
+    level_of(0, slopes)
     arrived(0, 1)
     level_of(1, scores)
-    arrived(1, 0)
-    level_of(0, slopes)
     arrived(0, 2)
     level_of(2, scores)
     arrived(0, 3)
@@ -311,14 +312,17 @@
         coef[chunk] = factors[chunk] / total
 
     def back(c, slot, dy):
-        src = terms.at[c, place(slot, dy)]
+        both = slot < 3
+        rows = place(slot, dy)
+        src = terms.at[:, rows] if both else terms.at[c, rows]
         if slot == 0:
-            dst, device = direct.at[c, -dy % NY], at(dy, 0)
+            dst, device = direct.at[:, -dy % NY], at(dy, 0)
         else:
             m, d = (3, dy // 2) if slot == 7 else divmod(slot - 1, 2)
             index = 12 + dy % 2 if slot == 7 else m * NY + -dy % NY
-            dst, device = relayed.at[c, d, index], at(dy, -m if d == 0 else m)
-        return remote(("back", c, slot, dy), src, dst, device)
+            dst = relayed.at[:, d, index] if both else relayed.at[c, d, index]
+            device = at(dy, -m if d == 0 else m)
+        return remote(("back", 0 if both else c, slot, dy), src, dst, device)
 
     def summed_copy(c, d):
         return remote(
@@ -338,27 +342,27 @@
         ds_buf[rows, :] = ds.astype(BF16)
         return mm(ds_buf[rows, :], qs[...]) * SCALE
 
-    def send_back(c, number):
-        def one(chunk):
-            terms[c, rows_of(chunk), :] = fill(c, chunk).astype(BF16)
-
-        level_of(number, one)
-        for slot in reversed(LEVELS[number]):
-            for dy in returned(slot):
-                go(back(c, slot, dy))
+    def send_back(c, slots):
+        for slot in slots:
+            terms[c, slot * SLOT : (slot + 1) * SLOT, :] = fill(c, slot).astype(BF16)
+            if slot > 2 or c == 0:
+                for dy in returned(slot):
+                    go(back(c, slot, dy))
 
     def mark(d, i, g):
         return marks[(d * 14 + i) * GROUPS + g]
 
+    def mine(c, slot):
+        return terms[c, slot * SLOT : slot * SLOT + BLOCK, :].astype(F32)
+
     def add_up(c):
         for d in range(2):
-            for slot in (7, 5 + d, 3 + d, 1 + d):
+            for slot in (7, 5 + d, 3 + d):
                 for dy in (2 * d, 2 * d + 1) if slot == 7 else returned(slot):
                     back(c, slot, dy).wait_recv()
 
             def one(g):
-                mine = terms[c, (1 + d) * SLOT : (1 + d) * SLOT + BLOCK, :]
-                result = mine.astype(F32) * mark(d, 0, g)
+                result = mine(c, 1 + d) * mark(d, 0, g)
                 for i in range(1, 14):
                     result = result + relayed[c, d, i].astype(F32) * mark(d, i, g)
                 summed[c, d, g] = result.astype(BF16)
@@ -366,21 +370,26 @@
             each_pair(GROUPS, one)
             go(summed_copy(c, d))
 
+    def add_up_own(c):
+        def one(g):
+            result = mine(c, 0) * mark(0, 0, g)
+            for dy in range(1, NY):
+                result = result + direct[c, dy].astype(F32) * mark(0, dy, g)
+            local[c, g] = result
+
+        each_pair(GROUPS, one)
+
     def finish(c):
-        for dy in returned(0):
-            back(c, 0, dy).wait_recv()
         for d in range(2):
             summed_copy(c, d).wait_recv()
         for slot in range(GROUPS):
             g = pg_ref[0, slot]
             result = back_in[c][0][g].astype(F32) + back_in[c][1][g].astype(F32)
-            result = result + terms[c, 0:BLOCK, :].astype(F32) * mark(0, 0, g)
-            for dy in range(1, NY):
-                result = result + direct[c, dy].astype(F32) * mark(0, dy, g)
-            op_ref[0, slot, :, c * HEAD : (c + 1) * HEAD] = result.astype(BF16)
-
-    send_back(1, 3)
-    send_back(1, 2)
+            op_ref[0, slot, :, c * HEAD : (c + 1) * HEAD] = (result + local[c, g]).astype(BF16)
+
+    sent_first = list(started)
+    started.clear()
+    send_back(1, (7, 5, 6, 3, 4))
     arrived(1, 1)
     level_of(1, slopes)
     arrived(1, 2)
@@ -391,12 +400,9 @@
     for chunk in range(1, LAST + 1):
         delta = delta + dots[chunk] * coef[chunk]
     row_delta[...] = delta
-    send_back(0, 3)
-    send_back(0, 2)
-    send_back(1, 1)
-    send_back(1, 0)
-    send_back(0, 1)
-    send_back(0, 0)
+    send_back(0, (7, 5, 6, 3, 4))
+    send_back(1, (1, 2, 0))
+    send_back(0, (1, 2, 0))
     listed = []
     for d, sign in ((0, 1), (1, -1)):
         for m in range(3):
@@ -405,12 +411,19 @@
     for n, group in enumerate(listed):
         for g in range(GROUPS):
             marks[n * GROUPS + g] = jnp.where(group == g, 1.0, 0.0).astype(F32)
+    for slot in (1, 2, 0):
+        for dy in returned(slot):
+            back(0, slot, dy).wait_recv()
+    add_up(1)
+    for copy in sent_first:
+        copy.wait_send()
     or_ref[:, HEAD:] = fill(1, LAST).astype(BF16)
     or_ref[:, :HEAD] = fill(0, LAST).astype(BF16)
-    add_up(1)
     dq = mm(kv[0].T, ds_buf[...]) * SCALE
     for h in range(HEADS):
         oq_ref[:, h * HEAD : (h + 1) * HEAD] = dq[:, h * HEAD : (h + 1) * HEAD].T.astype(BF16)
+    add_up_own(1)
+    add_up_own(0)
     add_up(0)
     finish(1)
     for copy in started:
@@ -435,7 +448,6 @@
     vmem = pl.BlockSpec(memory_space=pltpu.VMEM)
     smem = pl.BlockSpec(memory_space=pltpu.SMEM)
     block = (BLOCK, HEAD)
-    square = (WIDTH, WIDTH)
 
     def space(*shape, kind=BF16):
         return pltpu.VMEM(shape, kind)
@@ -446,10 +458,8 @@
     scratch = [
         space(*queries.shape),
         space(*prompt_kv.shape),
-        space(*grad_out.shape),
-        space(PIECES, *square),
-        space(NX, TOKENS, WIDTH),
-        space(NX, TOKENS, WIDTH),
+        space(NX, WIDTH, 2 * WIDTH),
+        space(NX, TOKENS, 2 * WIDTH),
         space(WIDTH, HEAD),
         space(WIDTH, HEAD),
         space(2, GROUPS, *block),
@@ -471,9 +481,10 @@
         space(2, NY, *block),
         space(2, 2, GROUPS, *block),
         streams(),
+        space(2, GROUPS, *block, kind=F32),
         pltpu.SMEM((28 * GROUPS,), F32),
         pltpu.SemaphoreType.DMA((5,)),
-        pltpu.SemaphoreType.DMA((PIECES,)),
+        pltpu.SemaphoreType.DMA((NX, 2)),
         pltpu.SemaphoreType.DMA((N_COPIES,)),
         pltpu.SemaphoreType.DMA((N_COPIES,)),
     ]

time: 55.5 us -> 57 us (1.027)
  Pallas kernels: 54.1 us -> 55.3 us
    pallas_call x1, Pallas kernels: 53.3 us -> 54.5 us  [body(): pl.pallas_call(kernel, out_shape=tuple((pltpu.VMEM(a.shape, BF16) for a i...]
where the time goes in v4:
time: 57 us; the launch traced here: 56.6 us
  Pallas kernels  55.3 us (97%)
  between operations  1.29 us (2%)
    pallas_call x1, Pallas kernels, body(): pl.pallas_call(kernel, out_shape=tuple((pltpu.VMEM(a.shape, BF16) for a i...  54.5 us

profile of v4, /device:TPU:2, one launch (start us, length us, event | category | flops | bytes accessed | tf_op | source)
XLA Modules:
  0.0 56.6 jit_solution(16492987464495737260)
XLA Ops:
  1.3 54.5 %shard_map.103 = (bf16[128,640]{1,0:T(8,128)(2,1)S(1)}, bf16[128,256]{1,0:T(8,128)(2,1)S(1)}, bf16[1,8,64,256]{3,2,1,0:T(8,128)(2,1)S(1)}) custom-call(bf16[128,640]{1,0:T(8,128)(2,1)} %q_ref.1, bf16[128,256]{1,0:T(8,128)(2,1)} %rkv_ref.1, bf16[1,8,64,256]{3,2,1,0:T(8,128)(2,1)} %pkv_ref.1, s32[1,8]{1,0:T(1,128)} %pg_ref.1, s32[32]{0:T(128)} %ro_ref.1, ...), custom_call_target="tpu_custom_call" | custom-call | flops 3000000000 | bytes 8000000 | tf_op jit(solution)/shard_map/pallas_call | solution.py:494
  55.8 0.8 %shard_map.104 = (bf16[128,640]{1,0:T(8,128)(2,1)}, bf16[128,256]{1,0:T(8,128)(2,1)}, bf16[1,8,64,256]{3,2,1,0:T(8,128)(2,1)}) custom-call(bf16[128,640]{1,0:T(8,128)(2,1)S(1)} %get-tuple-element.6.refs_0_, bf16[128,256]{1,0:T(8,128)(2,1)S(1)} %get-tuple-element.7.refs_1_, bf16[1,8,64,256]{3,2,1,0:T(8,128)(2,1)S(1)} %get-tuple-element.8.refs_2_), custom_call_target="tpu_custom_call" | custom-call | tf_op jit(solution)/shard_map/pallas_call | solution.py:511

commit v5 on v4

--- a/solution.py
+++ b/solution.py
@@ -116,6 +116,17 @@
     for copy in in_copies[1:]:
         copy.start()
 
+    w_copies = {}
+    for r in (0, 1, 3, 2):
+        for other in range(2):
+            piece = lax.rem(x + r, NX) * 2 + (core if other == 0 else 1 - core)
+            copy = pltpu.make_async_copy(
+                w_ref.at[:, pl.ds(pl.multiple_of(piece * WIDTH, WIDTH), WIDTH)],
+                w_v.at[r, :, pl.ds(other * WIDTH, WIDTH)], w_sem.at[r, other],
+            )
+            copy.start()
+            w_copies[r, other] = copy
+
     slot_of = []
     for g in range(GROUPS):
         slot = jnp.int32(0)
@@ -201,20 +212,8 @@
             go(x_copy(way, way if part == 0 else 1 - way))
     go(share(0))
 
-    w_copies = {}
-    for r in (0, 1, 3, 2):
-        for other in range(2):
-            piece = lax.rem(x + r, NX) * 2 + (core if other == 0 else 1 - core)
-            copy = pltpu.make_async_copy(
-                w_ref.at[:, pl.ds(pl.multiple_of(piece * WIDTH, WIDTH), WIDTH)],
-                w_v.at[r, :, pl.ds(other * WIDTH, WIDTH)], w_sem.at[r, other],
-            )
-            copy.start()
-            w_copies[r, other] = copy
     for g in range(GROUPS):
         own[1, g] = pkv_v[0, slot_of[g], :, HEAD:]
-    for d in range(2):
-        go(first_hop(1, d))
 
     groups = {
         dz: [lax.div(ro_ref[places[dy, dz]], 4) for dy in range(NY)] for dz in range(-3, 4)
@@ -266,6 +265,8 @@
         qs[h * HEAD : (h + 1) * HEAD, :] = q_v[:, h * HEAD : (h + 1) * HEAD]
     scores(LAST)
     share(0).wait_recv()
+    for d in range(2):
+        go(first_hop(1, d))
     grad = project(0)
     for way in range(2):
         x_copy(way, way).wait_recv()
@@ -276,14 +277,16 @@
         go(share(1 if way == 0 else 3))
     arrived(0, 0)
     level_of(0, scores)
+    share(1).wait_recv()
+    grad = grad + project(1)
     for way in range(2):
         x_pass(way).wait_recv()
     go(share(2))
-    share(1).wait_recv()
-    grad = grad + project(1)
     relay(1)
     share(3).wait_recv()
     grad = grad + project(3)
+    arrived(0, 1)
+    level_of(1, scores)
     share(2).wait_recv()
     grad = grad + project(2)
     column = lax.broadcasted_iota(jnp.int32, grad.shape, 1)
@@ -294,8 +297,6 @@
 
     slopes(LAST)
     level_of(0, slopes)
-    arrived(0, 1)
-    level_of(1, scores)
     arrived(0, 2)
     level_of(2, scores)
     arrived(0, 3)
@@ -312,7 +313,7 @@
         coef[chunk] = factors[chunk] / total
 
     def back(c, slot, dy):
-        both = slot < 3
+        both = slot == 0
         rows = place(slot, dy)
         src = terms.at[:, rows] if both else terms.at[c, rows]
         if slot == 0:
@@ -345,7 +346,7 @@
     def send_back(c, slots):
         for slot in slots:
             terms[c, slot * SLOT : (slot + 1) * SLOT, :] = fill(c, slot).astype(BF16)
-            if slot > 2 or c == 0:
+            if slot > 0 or c == 0:
                 for dy in returned(slot):
                     go(back(c, slot, dy))
 
@@ -357,7 +358,7 @@
 
     def add_up(c):
         for d in range(2):
-            for slot in (7, 5 + d, 3 + d):
+            for slot in (7, 5 + d, 3 + d, 1 + d):
                 for dy in (2 * d, 2 * d + 1) if slot == 7 else returned(slot):
                     back(c, slot, dy).wait_recv()
 
@@ -387,8 +388,14 @@
             result = back_in[c][0][g].astype(F32) + back_in[c][1][g].astype(F32)
             op_ref[0, slot, :, c * HEAD : (c + 1) * HEAD] = (result + local[c, g]).astype(BF16)
 
-    sent_first = list(started)
-    started.clear()
+    listed = []
+    for d, sign in ((0, 1), (1, -1)):
+        for m in range(3):
+            listed += groups[sign * m]
+        listed += [groups[sign * 3][-dy % NY] for dy in (2 * d, 2 * d + 1)]
+    for n, group in enumerate(listed):
+        for g in range(GROUPS):
+            marks[n * GROUPS + g] = jnp.where(group == g, 1.0, 0.0).astype(F32)
     send_back(1, (7, 5, 6, 3, 4))
     arrived(1, 1)
     level_of(1, slopes)
@@ -401,30 +408,21 @@
         delta = delta + dots[chunk] * coef[chunk]
     row_delta[...] = delta
     send_back(0, (7, 5, 6, 3, 4))
-    send_back(1, (1, 2, 0))
-    send_back(0, (1, 2, 0))
-    listed = []
-    for d, sign in ((0, 1), (1, -1)):
-        for m in range(3):
-            listed += groups[sign * m]
-        listed += [groups[sign * 3][-dy % NY] for dy in (2 * d, 2 * d + 1)]
-    for n, group in enumerate(listed):
-        for g in range(GROUPS):
-            marks[n * GROUPS + g] = jnp.where(group == g, 1.0, 0.0).astype(F32)
-    for slot in (1, 2, 0):
-        for dy in returned(slot):
-            back(0, slot, dy).wait_recv()
+    send_back(1, (1, 2))
+    send_back(0, (1, 2))
     add_up(1)
-    for copy in sent_first:
-        copy.wait_send()
+    add_up(0)
+    send_back(1, (0,))
+    send_back(0, (0,))
     or_ref[:, HEAD:] = fill(1, LAST).astype(BF16)
     or_ref[:, :HEAD] = fill(0, LAST).astype(BF16)
     dq = mm(kv[0].T, ds_buf[...]) * SCALE
     for h in range(HEADS):
         oq_ref[:, h * HEAD : (h + 1) * HEAD] = dq[:, h * HEAD : (h + 1) * HEAD].T.astype(BF16)
+    for dy in returned(0):
+        back(0, 0, dy).wait_recv()
     add_up_own(1)
     add_up_own(0)
-    add_up(0)
     finish(1)
     for copy in started:
         copy.wait_send()

time: 57 us -> 55.4 us (0.972)
  Pallas kernels: 55.3 us -> 54 us
    pallas_call x1, Pallas kernels: 54.5 us -> 53.2 us  [body(): pl.pallas_call(kernel, out_shape=tuple((pltpu.VMEM(a.shape, BF16) for a i...]
where the time goes in v5:
time: 55.4 us; the launch traced here: 55.3 us
  Pallas kernels  54 us (97%)
  between operations  1.29 us (2%)
    pallas_call x1, Pallas kernels, body(): pl.pallas_call(kernel, out_shape=tuple((pltpu.VMEM(a.shape, BF16) for a i...  53.2 us

profile of v5, /device:TPU:2, one launch (start us, length us, event | category | flops | bytes accessed | tf_op | source)
XLA Modules:
  0.0 55.3 jit_solution(12236924180924184937)
XLA Ops:
  1.3 53.2 %shard_map.103 = (bf16[128,640]{1,0:T(8,128)(2,1)S(1)}, bf16[128,256]{1,0:T(8,128)(2,1)S(1)}, bf16[1,8,64,256]{3,2,1,0:T(8,128)(2,1)S(1)}) custom-call(bf16[128,640]{1,0:T(8,128)(2,1)} %q_ref.1, bf16[128,256]{1,0:T(8,128)(2,1)} %rkv_ref.1, bf16[1,8,64,256]{3,2,1,0:T(8,128)(2,1)} %pkv_ref.1, s32[1,8]{1,0:T(1,128)} %pg_ref.1, s32[32]{0:T(128)} %ro_ref.1, ...), custom_call_target="tpu_custom_call" | custom-call | flops 3000000000 | bytes 8000000 | tf_op jit(solution)/shard_map/pallas_call | solution.py:492
  54.5 0.8 %shard_map.104 = (bf16[128,640]{1,0:T(8,128)(2,1)}, bf16[128,256]{1,0:T(8,128)(2,1)}, bf16[1,8,64,256]{3,2,1,0:T(8,128)(2,1)}) custom-call(bf16[128,640]{1,0:T(8,128)(2,1)S(1)} %get-tuple-element.6.refs_0_, bf16[128,256]{1,0:T(8,128)(2,1)S(1)} %get-tuple-element.7.refs_1_, bf16[1,8,64,256]{3,2,1,0:T(8,128)(2,1)S(1)} %get-tuple-element.8.refs_2_), custom_call_target="tpu_custom_call" | custom-call | tf_op jit(solution)/shard_map/pallas_call | solution.py:509

commit v6 on v5

--- a/solution.py
+++ b/solution.py
@@ -165,12 +165,13 @@
 
     def relay(c):
         for d in range(2):
-            sign = 1 if d == 0 else -1
             first_hop(c, d).wait_recv()
-            for m in (3, 2, 1, 0):
-                for dy in sent(d, m):
-                    picked[c, d, m, dy] = r1[c][d][groups[sign * m][dy]]
+        for m in (3, 2, 1, 0):
+            for pair in zip(sent(0, m), sent(1, m)):
+                for d, dy in enumerate(pair):
+                    picked[c, d, m, dy] = r1[c][d][groups[m if d == 0 else -m][dy]]
                     go(forward(c, d, m, dy))
+        for d in range(2):
             kv[c, (1 + d) * SLOT : (1 + d) * SLOT + BLOCK, :] = r1[c][d][groups[0][0]]
 
     def arrived(c, level):
@@ -325,9 +326,11 @@
             device = at(dy, -m if d == 0 else m)
         return remote(("back", 0 if both else c, slot, dy), src, dst, device)
 
-    def summed_copy(c, d):
+    def summed_copy(c, d, part):
+        groups_of = pl.ds(part * GROUPS // 2, GROUPS // 2)
         return remote(
-            ("summed", c, d), summed.at[c, d], back_in[c][d], at(0, -1 if d == 0 else 1)
+            ("summed", c, d, part), summed.at[c, d, groups_of], back_in[c][d].at[groups_of],
+            at(0, -1 if d == 0 else 1),
         )
 
     def returned(slot):
@@ -346,8 +349,11 @@
     def send_back(c, slots):
         for slot in slots:
             terms[c, slot * SLOT : (slot + 1) * SLOT, :] = fill(c, slot).astype(BF16)
-            if slot > 0 or c == 0:
-                for dy in returned(slot):
+        if slots == (0,) and c == 1:
+            return
+        for dy in (0, 2, 1, 3):
+            for slot in slots:
+                if dy in returned(slot):
                     go(back(c, slot, dy))
 
     def mark(d, i, g):
@@ -361,15 +367,18 @@
             for slot in (7, 5 + d, 3 + d, 1 + d):
                 for dy in (2 * d, 2 * d + 1) if slot == 7 else returned(slot):
                     back(c, slot, dy).wait_recv()
-
-            def one(g):
-                result = mine(c, 1 + d) * mark(d, 0, g)
-                for i in range(1, 14):
-                    result = result + relayed[c, d, i].astype(F32) * mark(d, i, g)
-                summed[c, d, g] = result.astype(BF16)
-
-            each_pair(GROUPS, one)
-            go(summed_copy(c, d))
+        for part in range(2):
+            for d in range(2):
+
+                def one(i):
+                    g = part * GROUPS // 2 + i
+                    result = mine(c, 1 + d) * mark(d, 0, g)
+                    for i in range(1, 14):
+                        result = result + relayed[c, d, i].astype(F32) * mark(d, i, g)
+                    summed[c, d, g] = result.astype(BF16)
+
+                each_pair(GROUPS // 2, one)
+                go(summed_copy(c, d, part))
 
     def add_up_own(c):
         def one(g):
@@ -381,8 +390,9 @@
         each_pair(GROUPS, one)
 
     def finish(c):
-        for d in range(2):
-            summed_copy(c, d).wait_recv()
+        for part in range(2):
+            for d in range(2):
+                summed_copy(c, d, part).wait_recv()
         for slot in range(GROUPS):
             g = pg_ref[0, slot]
             result = back_in[c][0][g].astype(F32) + back_in[c][1][g].astype(F32)
@@ -396,7 +406,8 @@
     for n, group in enumerate(listed):
         for g in range(GROUPS):
             marks[n * GROUPS + g] = jnp.where(group == g, 1.0, 0.0).astype(F32)
-    send_back(1, (7, 5, 6, 3, 4))
+    for slots in ((7,), (5, 6), (3, 4)):
+        send_back(1, slots)
     arrived(1, 1)
     level_of(1, slopes)
     arrived(1, 2)
@@ -407,7 +418,8 @@
     for chunk in range(1, LAST + 1):
         delta = delta + dots[chunk] * coef[chunk]
     row_delta[...] = delta
-    send_back(0, (7, 5, 6, 3, 4))
+    for slots in ((7,), (5, 6), (3, 4)):
+        send_back(0, slots)
     send_back(1, (1, 2))
     send_back(0, (1, 2))
     add_up(1)

time: 55.4 us -> 55.1 us (level)
  no operation moved by 1% of the time
where the time goes in v6:
time: 55.1 us; the launch traced here: 54.9 us
  Pallas kernels  53.7 us (97%)
  between operations  1.29 us (2%)
    pallas_call x1, Pallas kernels, body(): pl.pallas_call(kernel, out_shape=tuple((pltpu.VMEM(a.shape, BF16) for a i...  52.9 us

profile of v6, /device:TPU:2, one launch (start us, length us, event | category | flops | bytes accessed | tf_op | source)
XLA Modules:
  0.0 54.9 jit_solution(13481896614619893771)
XLA Ops:
  1.3 52.9 %shard_map.103 = (bf16[128,640]{1,0:T(8,128)(2,1)S(1)}, bf16[128,256]{1,0:T(8,128)(2,1)S(1)}, bf16[1,8,64,256]{3,2,1,0:T(8,128)(2,1)S(1)}) custom-call(bf16[128,640]{1,0:T(8,128)(2,1)} %q_ref.1, bf16[128,256]{1,0:T(8,128)(2,1)} %rkv_ref.1, bf16[1,8,64,256]{3,2,1,0:T(8,128)(2,1)} %pkv_ref.1, s32[1,8]{1,0:T(1,128)} %pg_ref.1, s32[32]{0:T(128)} %ro_ref.1, ...), custom_call_target="tpu_custom_call" | custom-call | flops 3000000000 | bytes 8000000 | tf_op jit(solution)/shard_map/pallas_call | solution.py:504
  54.1 0.8 %shard_map.104 = (bf16[128,640]{1,0:T(8,128)(2,1)}, bf16[128,256]{1,0:T(8,128)(2,1)}, bf16[1,8,64,256]{3,2,1,0:T(8,128)(2,1)}) custom-call(bf16[128,640]{1,0:T(8,128)(2,1)S(1)} %get-tuple-element.6.refs_0_, bf16[128,256]{1,0:T(8,128)(2,1)S(1)} %get-tuple-element.7.refs_1_, bf16[1,8,64,256]{3,2,1,0:T(8,128)(2,1)S(1)} %get-tuple-element.8.refs_2_), custom_call_target="tpu_custom_call" | custom-call | tf_op jit(solution)/shard_map/pallas_call | solution.py:521

commit v7 on v6

--- a/solution.py
+++ b/solution.py
@@ -136,8 +136,6 @@
     in_copies[0].wait()
     for g in range(GROUPS):
         own[0, g] = pkv_v[0, slot_of[g], :, :HEAD]
-    for copy in in_copies[1:]:
-        copy.wait()
     pl.semaphore_wait(barrier, len(partners))
 
     def first_hop(c, d):
@@ -208,6 +206,8 @@
 
     for d in range(2):
         go(first_hop(0, d))
+    for copy in in_copies[1:]:
+        copy.wait()
     for part in range(2):
         for way in range(2):
             go(x_copy(way, way if part == 0 else 1 - way))
@@ -215,6 +215,8 @@
 
     for g in range(GROUPS):
         own[1, g] = pkv_v[0, slot_of[g], :, HEAD:]
+    for d in range(2):
+        go(first_hop(1, d))
 
     groups = {
         dz: [lax.div(ro_ref[places[dy, dz]], 4) for dy in range(NY)] for dz in range(-3, 4)
@@ -266,8 +268,6 @@
         qs[h * HEAD : (h + 1) * HEAD, :] = q_v[:, h * HEAD : (h + 1) * HEAD]
     scores(LAST)
     share(0).wait_recv()
-    for d in range(2):
-        go(first_hop(1, d))
     grad = project(0)
     for way in range(2):
         x_copy(way, way).wait_recv()
@@ -276,6 +276,7 @@
     for way in range(2):
         x_copy(way, 1 - way).wait_recv()
         go(share(1 if way == 0 else 3))
+    relay(1)
     arrived(0, 0)
     level_of(0, scores)
     share(1).wait_recv()
@@ -283,7 +284,6 @@
     for way in range(2):
         x_pass(way).wait_recv()
     go(share(2))
-    relay(1)
     share(3).wait_recv()
     grad = grad + project(3)
     arrived(0, 1)

time: 55.1 us -> 55.1 us (level)
  no operation moved by 1% of the time
where the time goes in v7:
time: 55.1 us; the launch traced here: 55 us
  Pallas kernels  53.7 us (97%)
  between operations  1.29 us (2%)
    pallas_call x1, Pallas kernels, body(): pl.pallas_call(kernel, out_shape=tuple((pltpu.VMEM(a.shape, BF16) for a i...  52.9 us

profile of v7, /device:TPU:2, one launch (start us, length us, event | category | flops | bytes accessed | tf_op | source)
XLA Modules:
  0.0 55.0 jit_solution(7603945824344393487)
XLA Ops:
  1.3 52.9 %shard_map.103 = (bf16[128,640]{1,0:T(8,128)(2,1)S(1)}, bf16[128,256]{1,0:T(8,128)(2,1)S(1)}, bf16[1,8,64,256]{3,2,1,0:T(8,128)(2,1)S(1)}) custom-call(bf16[128,640]{1,0:T(8,128)(2,1)} %q_ref.1, bf16[128,256]{1,0:T(8,128)(2,1)} %rkv_ref.1, bf16[1,8,64,256]{3,2,1,0:T(8,128)(2,1)} %pkv_ref.1, s32[1,8]{1,0:T(1,128)} %pg_ref.1, s32[32]{0:T(128)} %ro_ref.1, ...), custom_call_target="tpu_custom_call" | custom-call | flops 3000000000 | bytes 8000000 | tf_op jit(solution)/shard_map/pallas_call | solution.py:504
  54.2 0.8 %shard_map.104 = (bf16[128,640]{1,0:T(8,128)(2,1)}, bf16[128,256]{1,0:T(8,128)(2,1)}, bf16[1,8,64,256]{3,2,1,0:T(8,128)(2,1)}) custom-call(bf16[128,640]{1,0:T(8,128)(2,1)S(1)} %get-tuple-element.6.refs_0_, bf16[128,256]{1,0:T(8,128)(2,1)S(1)} %get-tuple-element.7.refs_1_, bf16[1,8,64,256]{3,2,1,0:T(8,128)(2,1)S(1)} %get-tuple-element.8.refs_2_), custom_call_target="tpu_custom_call" | custom-call | tf_op jit(solution)/shard_map/pallas_call | solution.py:521

commit v8 on v7

--- a/solution.py
+++ b/solution.py
@@ -59,7 +59,7 @@
     oq_ref, or_ref, op_ref,
     q_v, pkv_v,
     w_v, gathered, qs, gs,
-    own, r1, picked, picked_own, kv,
+    own, r1, picked, picked_own, kv, keys_turned,
     e_buf, p_buf, dp_buf, ds_buf,
     tops, sums, dots, coef, row_delta,
     terms, relayed, direct, summed, back_in, local,
@@ -276,6 +276,8 @@
     for way in range(2):
         x_copy(way, 1 - way).wait_recv()
         go(share(1 if way == 0 else 3))
+    early = list(started)
+    started.clear()
     relay(1)
     arrived(0, 0)
     level_of(0, scores)
@@ -339,8 +341,7 @@
     def fill(c, chunk):
         rows = rows_of(chunk)
         if c == 1:
-            p = e_buf[rows, :].astype(F32) * coef[chunk]
-            p_buf[rows, :] = p.astype(BF16)
+            p_buf[rows, :] = e_buf[rows, :] * coef[chunk].astype(BF16)
             return mm(p_buf[rows, :], gs[...])
         ds = p_buf[rows, :].astype(F32) * (dp_buf[rows, :] - row_delta[...])
         ds_buf[rows, :] = ds.astype(BF16)
@@ -408,6 +409,9 @@
             marks[n * GROUPS + g] = jnp.where(group == g, 1.0, 0.0).astype(F32)
     for slots in ((7,), (5, 6), (3, 4)):
         send_back(1, slots)
+    keys_turned[...] = kv[0].T
+    for copy in early:
+        copy.wait_send()
     arrived(1, 1)
     level_of(1, slopes)
     arrived(1, 2)
@@ -423,12 +427,12 @@
     send_back(1, (1, 2))
     send_back(0, (1, 2))
     add_up(1)
+    or_ref[:, HEAD:] = fill(1, LAST).astype(BF16)
+    or_ref[:, :HEAD] = fill(0, LAST).astype(BF16)
     add_up(0)
     send_back(1, (0,))
     send_back(0, (0,))
-    or_ref[:, HEAD:] = fill(1, LAST).astype(BF16)
-    or_ref[:, :HEAD] = fill(0, LAST).astype(BF16)
-    dq = mm(kv[0].T, ds_buf[...]) * SCALE
+    dq = mm(keys_turned[...], ds_buf[...]) * SCALE
     for h in range(HEADS):
         oq_ref[:, h * HEAD : (h + 1) * HEAD] = dq[:, h * HEAD : (h + 1) * HEAD].T.astype(BF16)
     for dy in returned(0):
@@ -477,6 +481,7 @@
         space(2, 2, 4, NY, *block),
         space(2, NY, *block),
         space(2, PROMPT + TOKENS, HEAD),
+        space(HEAD, PROMPT + TOKENS),
         space(PROMPT + TOKENS, WIDTH),
         space(PROMPT + TOKENS, WIDTH),
         space(PROMPT + TOKENS, WIDTH, kind=F32),

time: 55.1 us -> 55 us (level)
  no operation moved by 1% of the time
where the time goes in v8:
time: 55 us; the launch traced here: 54.9 us
  Pallas kernels  53.6 us (97%)
  between operations  1.29 us (2%)
    pallas_call x1, Pallas kernels, body(): pl.pallas_call(kernel, out_shape=tuple((pltpu.VMEM(a.shape, BF16) for a i...  52.8 us

profile of v8, /device:TPU:2, one launch (start us, length us, event | category | flops | bytes accessed | tf_op | source)
XLA Modules:
  0.0 54.9 jit_solution(12560071668094847371)
XLA Ops:
  1.3 52.8 %shard_map.103 = (bf16[128,640]{1,0:T(8,128)(2,1)S(1)}, bf16[128,256]{1,0:T(8,128)(2,1)S(1)}, bf16[1,8,64,256]{3,2,1,0:T(8,128)(2,1)S(1)}) custom-call(bf16[128,640]{1,0:T(8,128)(2,1)} %q_ref.1, bf16[128,256]{1,0:T(8,128)(2,1)} %rkv_ref.1, bf16[1,8,64,256]{3,2,1,0:T(8,128)(2,1)} %pkv_ref.1, s32[1,8]{1,0:T(1,128)} %pg_ref.1, s32[32]{0:T(128)} %ro_ref.1, ...), custom_call_target="tpu_custom_call" | custom-call | flops 3000000000 | bytes 8000000 | tf_op jit(solution)/shard_map/pallas_call | solution.py:509
  54.1 0.8 %shard_map.104 = (bf16[128,640]{1,0:T(8,128)(2,1)}, bf16[128,256]{1,0:T(8,128)(2,1)}, bf16[1,8,64,256]{3,2,1,0:T(8,128)(2,1)}) custom-call(bf16[128,640]{1,0:T(8,128)(2,1)S(1)} %get-tuple-element.6.refs_0_, bf16[128,256]{1,0:T(8,128)(2,1)S(1)} %get-tuple-element.7.refs_1_, bf16[1,8,64,256]{3,2,1,0:T(8,128)(2,1)S(1)} %get-tuple-element.8.refs_2_), custom_call_target="tpu_custom_call" | custom-call | tf_op jit(solution)/shard_map/pallas_call | solution.py:526

commit v9 on v8

--- a/solution.py
+++ b/solution.py
@@ -52,6 +52,7 @@
 
 LEVELS = [(0,), (1, 2), (3, 4), (5, 6, 7)]
 LAST = 8
+REACH = (0, 0, 1, 2)
 
 
 def kernel(
@@ -59,7 +60,7 @@
     oq_ref, or_ref, op_ref,
     q_v, pkv_v,
     w_v, gathered, qs, gs,
-    own, r1, picked, picked_own, kv, keys_turned,
+    own, r1, r2, picked, picked_own, kv, keys_turned,
     e_buf, p_buf, dp_buf, ds_buf,
     tops, sums, dots, coef, row_delta,
     terms, relayed, direct, summed, back_in, local,
@@ -141,6 +142,9 @@
     def first_hop(c, d):
         return remote(("first", c, d), own.at[c], r1[c][d], at(0, 1 if d == 0 else -1))
 
+    def second_hop(c, d):
+        return remote(("second", c, d), r1[c][d], r2[c][d], at(0, 1 if d == 0 else -1))
+
     def place(slot, dy):
         return pl.ds(slot * SLOT + (dy % NY) * BLOCK, BLOCK)
 
@@ -153,24 +157,35 @@
         slot = 7 if m == 3 else 1 + d + 2 * m
         return remote(
             ("forward", c, d, m, dy), picked.at[c, d, m, dy], kv.at[c, place(slot, -dy)],
-            at(dy, m if d == 0 else -m),
+            at(dy, REACH[m] if d == 0 else -REACH[m]),
         )
 
     def sent(d, m):
         if m == 3:
             return (2 * d, 2 * d + 1)
-        return (1, 2, 3) if m == 0 else (0, 1, 2, 3)
-
-    def relay(c):
+        return (1, 2, 3) if m < 2 else (0, 1, 2, 3)
+
+    def pick(c, m, src):
+        for pair in zip(sent(0, m), sent(1, m)):
+            for d, dy in enumerate(pair):
+                picked[c, d, m, dy] = src[c][d][groups[REACH[m] if d == 0 else -REACH[m]][dy]]
+                go(forward(c, d, m, dy))
+
+    def relay_near(c):
         for d in range(2):
             first_hop(c, d).wait_recv()
-        for m in (3, 2, 1, 0):
-            for pair in zip(sent(0, m), sent(1, m)):
-                for d, dy in enumerate(pair):
-                    picked[c, d, m, dy] = r1[c][d][groups[m if d == 0 else -m][dy]]
-                    go(forward(c, d, m, dy))
+            go(second_hop(c, d))
+        pick(c, 0, r1)
         for d in range(2):
             kv[c, (1 + d) * SLOT : (1 + d) * SLOT + BLOCK, :] = r1[c][d][groups[0][0]]
+
+    def relay_far(c):
+        for d in range(2):
+            second_hop(c, d).wait_recv()
+        for m in (3, 2, 1):
+            pick(c, m, r2)
+        for d in range(2):
+            kv[c, (3 + d) * SLOT : (3 + d) * SLOT + BLOCK, :] = r2[c][d][groups[0][0]]
 
     def arrived(c, level):
         if level == 0:
@@ -272,13 +287,13 @@
     for way in range(2):
         x_copy(way, way).wait_recv()
         go(x_pass(way))
-    relay(0)
+    relay_near(0)
     for way in range(2):
         x_copy(way, 1 - way).wait_recv()
         go(share(1 if way == 0 else 3))
     early = list(started)
     started.clear()
-    relay(1)
+    relay_near(1)
     arrived(0, 0)
     level_of(0, scores)
     share(1).wait_recv()
@@ -290,6 +305,7 @@
     grad = grad + project(3)
     arrived(0, 1)
     level_of(1, scores)
+    relay_far(0)
     share(2).wait_recv()
     grad = grad + project(2)
     column = lax.broadcasted_iota(jnp.int32, grad.shape, 1)
@@ -300,6 +316,7 @@
 
     slopes(LAST)
     level_of(0, slopes)
+    relay_far(1)
     arrived(0, 2)
     level_of(2, scores)
     arrived(0, 3)
@@ -477,6 +494,7 @@
         space(WIDTH, HEAD),
         space(WIDTH, HEAD),
         space(2, GROUPS, *block),
+        streams(),
         streams(),
         space(2, 2, 4, NY, *block),
         space(2, NY, *block),

time: 55 us -> 56.5 us (1.027)
  Pallas kernels: 53.6 us -> 55 us
    pallas_call x1, Pallas kernels: 52.8 us -> 54.2 us  [body(): pl.pallas_call(kernel, out_shape=tuple((pltpu.VMEM(a.shape, BF16) for a i...]
where the time goes in v9:
time: 56.5 us; the launch traced here: 56.3 us
  Pallas kernels  55 us (97%)
  between operations  1.29 us (2%)
    pallas_call x1, Pallas kernels, body(): pl.pallas_call(kernel, out_shape=tuple((pltpu.VMEM(a.shape, BF16) for a i...  54.2 us

profile of v9, /device:TPU:2, one launch (start us, length us, event | category | flops | bytes accessed | tf_op | source)
XLA Modules:
  0.0 56.3 jit_solution(17371950962190763789)
XLA Ops:
  1.3 54.2 %shard_map.103 = (bf16[128,640]{1,0:T(8,128)(2,1)S(1)}, bf16[128,256]{1,0:T(8,128)(2,1)S(1)}, bf16[1,8,64,256]{3,2,1,0:T(8,128)(2,1)S(1)}) custom-call(bf16[128,640]{1,0:T(8,128)(2,1)} %q_ref.1, bf16[128,256]{1,0:T(8,128)(2,1)} %rkv_ref.1, bf16[1,8,64,256]{3,2,1,0:T(8,128)(2,1)} %pkv_ref.1, s32[1,8]{1,0:T(1,128)} %pg_ref.1, s32[32]{0:T(128)} %ro_ref.1, ...), custom_call_target="tpu_custom_call" | custom-call | flops 3000000000 | bytes 8000000 | tf_op jit(solution)/shard_map/pallas_call | solution.py:527
  55.5 0.8 %shard_map.104 = (bf16[128,640]{1,0:T(8,128)(2,1)}, bf16[128,256]{1,0:T(8,128)(2,1)}, bf16[1,8,64,256]{3,2,1,0:T(8,128)(2,1)}) custom-call(bf16[128,640]{1,0:T(8,128)(2,1)S(1)} %get-tuple-element.6.refs_0_, bf16[128,256]{1,0:T(8,128)(2,1)S(1)} %get-tuple-element.7.refs_1_, bf16[1,8,64,256]{3,2,1,0:T(8,128)(2,1)S(1)} %get-tuple-element.8.refs_2_), custom_call_target="tpu_custom_call" | custom-call | tf_op jit(solution)/shard_map/pallas_call | solution.py:544
